TPU v7x, 256 devices: a whole 4x4x8 slice. The times are simulated.
256 devices in a mesh: sky: 32 (over y, x, core), gz: 8 (over z).
Axes of the slice: x: 4, y: 4, z: 8, core: 2. Of those that a mesh axis runs over, the one named last changes fastest.
Arguments:
- delta_flux: float32 [32, 8, 32, 128], P('sky', 'gz'), may hold values from -6 to 6
- noise_var: float32 [32, 8, 32, 128], P('sky', 'gz'), may hold values from 0.5 to 2
- pixel_pos: float32 [32, 8, 3, 32, 128], P('sky', 'gz'), may hold values from 0 to 64, as said below
- pixel_count: int32 [32, 8, 32], P('sky', 'gz'), may hold values from 1 to 128, as said below
- pair_list: int32 [32, 8, 3, 128], P('sky', 'gz'), may hold values from 0 to 31, as said below
Outputs:
- wiener_field: float32 [32, 8, 32, 128], P('sky', 'gz')
- residual: float32 [32, 8, 32, 128], P('sky', 'gz')
Inputs may be any that keep to these rules, and one draw needn't show every extreme that they name: pair_list[t, g, 0, k] is a neighbour code 3 (a + 1) + (b + 1) for a sky offset a and a redshift offset b in -1..1, or 9 for an empty slot; rows 1 and 2 are block numbers below 32. On every tile the filled slots come first, sorted by code; their number differs from tile to tile and one tile fills all 128 slots. `pixel_count`: every tile and segment has a block with all 128 pixels live. `pixel_pos`: component 0 of tile t lies in [2 t, 2 t + 2], component 1 in [0, 2], component 2 of segment g in [4 g, 4 g + 4].
All inputs are finite; a program needn't handle non-finite values.
Results may differ from a plain program's by a relative error of at most 0.00075.
Values sent between devices are 32-bit elements; how exact they have to be, the bound alone decides.
A program may use at most 128 MiB of HBM per device.

v0:
```python
import jax
import jax.numpy as jnp
from jax import lax
from jax.sharding import PartitionSpec as P

GROUP = 32
ITERS = 3


signal_amp = 0.25
spread_inv = 0.5


def shifted(block, axis, distance):
    devices = range(lax.axis_size(axis))
    route = [(i - distance, i) for i in devices if i - distance in devices]
    return lax.ppermute(block, axis, route)


def padded(block, sides, width):
    for axis, dim in sides:
        count = lax.axis_size(axis)
        forward = [(i, i + 1) for i in range(count - 1)]
        backward = [(target, source) for source, target in forward]
        low = lax.ppermute(
            lax.slice_in_dim(block, block.shape[dim] - width, None, axis=dim), axis, forward
        )
        high = lax.ppermute(lax.slice_in_dim(block, 0, width, axis=dim), axis, backward)
        block = jnp.concatenate([low, block, high], axis=dim)
    return block


def kernel_tiles(left_pos, right_pos):
    diff_x = left_pos[:, 0, :, None] - right_pos[:, 0, None, :]
    diff_y = left_pos[:, 1, :, None] - right_pos[:, 1, None, :]
    diff_z = left_pos[:, 2, :, None] - right_pos[:, 2, None, :]
    squared = diff_x * diff_x + diff_y * diff_y + diff_z * diff_z
    return signal_amp * jnp.exp(-spread_inv * squared)


def apply_tiles(tiles, vectors):
    return jnp.einsum("gab,gb->ga", tiles, vectors, precision=lax.Precision.HIGHEST)


def apply_trans(tiles, vectors):
    return jnp.einsum("gab,ga->gb", tiles, vectors, precision=lax.Precision.HIGHEST)


def scatter_rows(rows, index, count):
    picker = (index[:, None] == lax.broadcasted_iota(jnp.int32, (index.shape[0], count), 1)).astype(
        jnp.float32
    )
    return jnp.einsum("gn,gb->nb", picker, rows, precision=lax.Precision.HIGHEST)


def pass_gz(values, offset):
    return shifted(values, "gz", offset)


def pass_sky(values, offset):
    return shifted(values, "sky", offset)


def rz_total(resid, precond_r):
    return lax.psum(jnp.sum(resid * precond_r), ("sky", "gz"))


def local(delta_flux, noise_var, pixel_pos, pixel_count, pair_list):
    blocks = delta_flux.shape[2]
    blk_width = delta_flux.shape[3]
    slot_count = pair_list.shape[3]
    group_count = slot_count // GROUP
    pos_local = jnp.transpose(pixel_pos, (0, 1, 3, 2, 4))
    pos_rim = padded(pos_local, (("sky", 0), ("gz", 1)), 1)
    pos_rim = pos_rim.reshape(9 * blocks, 3, blk_width)
    pos_own = pos_local[0, 0]
    live_mask = (
        lax.broadcasted_iota(jnp.int32, (blocks, blk_width), 1) < pixel_count[0, 0][:, None]
    ).astype(jnp.float32)
    noise_own = noise_var[0, 0]
    precond = 1.0 / (noise_own + signal_amp)
    self_tiles = kernel_tiles(pos_own, pos_own)
    own_list = pair_list[0, 0]
    all_codes = own_list[0]
    all_source = own_list[1]
    all_target = own_list[2]
    all_weight = (all_codes < 9).astype(jnp.float32)
    all_flat = jnp.minimum(all_codes, 8) * blocks + all_source
    live_count = jnp.sum((all_codes < 9).astype(jnp.int32))
    own_groups = (live_count + GROUP - 1) // GROUP
    self_count = scatter_rows(all_weight[:, None], all_target, blocks)

    def cross_group(pieces):
        near_pos = pos_own[pieces[1]]
        far_pos = pos_rim[pieces[0]]
        return pieces[2][:, None, None] * kernel_tiles(near_pos, far_pos)

    grouped = (
        all_flat.reshape(group_count, GROUP),
        all_target.reshape(group_count, GROUP),
        all_weight.reshape(group_count, GROUP),
    )
    cross_all = lax.map(cross_group, grouped).reshape(slot_count, blk_width, blk_width)

    def far_group(pieces):
        far_pos = pos_rim[pieces[0]]
        return pieces[2][:, None, None] * kernel_tiles(far_pos, far_pos)

    far_all = lax.map(far_group, grouped).reshape(slot_count, blk_width, blk_width)
    right_side = live_mask * delta_flux[0, 0]
    wiener_field = jnp.zeros_like(right_side)
    residual = right_side
    precond_res = precond * residual
    direction = precond_res
    rz_now = rz_total(residual, precond_res)
    for iteration in range(ITERS):
        vector = direction
        halo_vec = padded(vector[None, None], (("sky", 0), ("gz", 1)), 1)
        halo_vec = halo_vec.reshape(9 * blocks, blk_width)
        totals = apply_tiles(self_tiles, vector) * (1.0 + self_count)

        def own_step(group_idx, carry):
            begin = group_idx * GROUP
            cross_tile = lax.dynamic_slice_in_dim(cross_all, begin, GROUP, 0)
            far_tile = lax.dynamic_slice_in_dim(far_all, begin, GROUP, 0)
            target = lax.dynamic_slice_in_dim(all_target, begin, GROUP, 0)
            flat_src = lax.dynamic_slice_in_dim(all_flat, begin, GROUP, 0)
            near_vec = vector[target]
            far_vec = halo_vec[flat_src]
            to_target = apply_tiles(cross_tile, far_vec)
            to_source = apply_trans(cross_tile, near_vec) + apply_tiles(far_tile, far_vec)
            return (
                carry[0] + scatter_rows(to_target, target, blocks),
                carry[1] + scatter_rows(to_source, flat_src, 9 * blocks),
            )

        start_carry = (
            jnp.zeros((blocks, blk_width), jnp.float32),
            jnp.zeros((9 * blocks, blk_width), jnp.float32),
        )
        gained, owed = lax.fori_loop(0, own_groups, own_step, start_carry)
        owed = owed.reshape(3, 3, blocks, blk_width)
        column = owed[:, 1] + pass_gz(owed[:, 2], 1) + pass_gz(owed[:, 0], -1)
        arrived = column[1] + pass_sky(column[2], 1) + pass_sky(column[0], -1)
        totals = totals + gained + arrived
        image = live_mask * totals + noise_own * vector
        step_len = rz_now / lax.psum(jnp.sum(direction * image), ("sky", "gz"))
        wiener_field = wiener_field + step_len * direction
        residual = residual - step_len * image
        precond_res = precond * residual
        rz_next = rz_total(residual, precond_res)
        direction = precond_res + rz_next / rz_now * direction
        rz_now = rz_next
    return (wiener_field[None, None], residual[None, None])


def solution(mesh):
    placed = (
        P("sky", "gz", None, None),
        P("sky", "gz", None, None),
        P("sky", "gz", None, None, None),
        P("sky", "gz", None),
        P("sky", "gz", None, None),
    )
    return jax.shard_map(
        local,
        mesh=mesh,
        in_specs=placed,
        out_specs=(P("sky", "gz", None, None), P("sky", "gz", None, None)),
        check_vma=False,
    )
```

profile of v0, /device:TPU:1, one launch (start us, length us, event | category | flops | bytes accessed | tf_op | source)
XLA Modules:
  0.0 754.1 jit_solution(13700068418464653946)
XLA Ops:
  1.4 4.5 collective-permute-start.4
  8.7 3.6 collective-permute-start
  18.3 3.5 collective-permute-start.6
  23.3 4.2 collective-permute-start.2
  31.1 4.1 collective-permute-done.3
  35.4 4.3 broadcast.293.clone
  39.7 17.9 %while.56 = (s32[]{:T(128)}, f32[4,32,128,128]{3,2,1,0:T(8,128)}, s32[4,32]{1,0:T(4,128)S(1)}, f32[32,3,128]{2,1,0:T(4,128)S(1)}, s32[4,32]{1,0:T(4,128)S(1)}, /...) while((s32[]{:T(128)}, f32[4,32,128,128]{3,2,1,0:T(8,128)}, s32[4,32]{1,0:T(4,128)S(1)}, ...), condition=%wide.region_4.5_spmd, body=%wide.region_3.4_spmd.sunk | while | flops 5245154 | bytes 2598877 | solution.py:103
  57.5 4.3 broadcast.293.clone.1
  61.8 15.2 %while.57 = (s32[]{:T(128)}, f32[4,32,128,128]{3,2,1,0:T(8,128)}, s32[4,32]{1,0:T(4,128)S(1)}, f32[288,3,128]{2,1,0:T(4,128)S(1)}, f32[4,32]{1,0:T(4,128)S(1)}, /*index=5*/s32[]{:T(128)}) while((s32[]{:T(128)}, f32[4,32,128,128]{3,2,1,0:T(8,128)}, s32[4,32]{1,0:T(4,128)S(1)}, f32[288,3,128]{2,1,0:T(4,128)S(1)}, f32[4,32]{1,0:T(4,128)S(1)}, ...), condition=%wide.region_6.7_spmd, body=%wide.region_5.6_spmd.sunk | while | flops 5244034 | bytes 2398029 | solution.py:109
  77.1 45.8 %while.58 = (s32[]{:T(128)}, f32[32,128]{1,0:T(8,128)S(1)}, f32[288,128]{1,0:T(8,128)S(1)}, s32[]{:T(128)}, s32[128]{0:T(128)S(1)}, /*index=5*/f32[128,128,128]{...) while((s32[]{:T(128)}, f32[32,128]{1,0:T(8,128)S(1)}, ...), condition=%wide.region_8.9_spmd, body=%wide.region_7.8_spmd.sunk | while | flops 34660548 | bytes 6842051 | solution.py:141
  81.8 4.9 fusion.188
  87.1 4.9 fusion.186
  97.1 4.9 fusion.188
  102.4 4.9 fusion.186
  112.3 4.9 fusion.188
  117.7 4.9 fusion.186
  122.9 4.6 collective-permute-start.8
  128.8 5.1 fusion.48
  139.2 16.9 %collective-permute-done.11 = f32[32,128]{1,0:T(8,128)S(1)} collective-permute-done((f32[32,128]{1,0:T(8,128)S(1)}, f32[32,128]{1,0:T(8,128)S(1)}, u32[]{:S(2)}, u32[]{:S(2)}) %collective-permute-start.11) | collective-permute-done | bytes 16416 | tf_op jit(solution)/shard_map/ppermute | solution.py:17
  156.8 88.7 %all-reduce = (f32[]{:T(128)}, f32[]{:T(128)}) all-reduce(f32[]{:T(128)} %get-tuple-element.237, f32[]{:T(128)} %get-tuple-element.236), channel_id=1, replica_groups=mesh['sky'=32,'gz'=8] {'sky','gz'}, use_global_device_ids=true, to_apply=%region_1.2 | all-reduce | flops 2 | bytes 16 | tf_op jit(solution)/shard_map/psum | solution.py:65
  247.5 73.5 %psum.44 = f32[]{:T(128)} all-reduce(f32[]{:T(128)} %get-tuple-element.342), channel_id=1, replica_groups=mesh['sky'=32,'gz'=8] {'sky','gz'}, use_global_device_ids=true, to_apply=%region_12.13 | all-reduce | flops 1 | bytes 8 | tf_op jit(solution)/shard_map/psum | solution.py:65
  330.8 3.6 collective-permute-start.14
  335.7 3.5 collective-permute-done.15
  339.3 45.8 %while.59 = (s32[]{:T(128)}, f32[32,128]{1,0:T(8,128)S(1)}, f32[288,128]{1,0:T(8,128)S(1)}, s32[]{:T(128)}, s32[128]{0:T(128)S(1)}, /*index=5*/f32[128,128,128]{...) while((s32[]{:T(128)}, f32[32,128]{1,0:T(8,128)S(1)}, ...), condition=%wide.region_14.15_spmd, body=%wide.region_13.14_spmd.sunk | while | flops 34660548 | bytes 6842051 | solution.py:141
  344.0 4.9 fusion.199
  349.4 4.9 fusion.197
  359.3 4.9 fusion.199
  364.6 4.9 fusion.197
  374.6 4.9 fusion.199
  379.9 4.9 fusion.197
  388.4 4.2 collective-permute-done.17
  396.9 5.1 fusion.47
  402.1 10.6 %collective-permute-done.19 = f32[32,128]{1,0:T(8,128)S(1)} collective-permute-done((f32[32,128]{1,0:T(8,128)S(1)}, f32[32,128]{1,0:T(8,128)S(1)}, u32[]{:S(2)}, u32[]{:S(2)}) %collective-permute-start.19) | collective-permute-done | bytes 16416 | tf_op jit(solution)/shard_map/ppermute | solution.py:17
  413.4 86.2 %psum.45 = f32[]{:T(128)} all-reduce(f32[]{:T(128)} %get-tuple-element.340), channel_id=1, replica_groups=mesh['sky'=32,'gz'=8] {'sky','gz'}, use_global_device_ids=true, to_apply=%region_16.17 | all-reduce | flops 1 | bytes 8 | tf_op jit(solution)/shard_map/psum | solution.py:147
  501.4 72.4 %psum.46 = f32[]{:T(128)} all-reduce(f32[]{:T(128)} %get-tuple-element.338), channel_id=1, replica_groups=mesh['sky'=32,'gz'=8] {'sky','gz'}, use_global_device_ids=true, to_apply=%region_18.19 | all-reduce | flops 1 | bytes 8 | tf_op jit(solution)/shard_map/psum | solution.py:65
  583.1 3.7 collective-permute-start.22
  588.1 3.5 collective-permute-done.23
  591.7 46.0 %while.60 = (s32[]{:T(128)}, f32[32,128]{1,0:T(8,128)S(1)}, f32[288,128]{1,0:T(8,128)S(1)}, s32[]{:T(128)}, s32[128]{0:T(128)S(1)}, /*index=5*/f32[128,128,128]{...) while((s32[]{:T(128)}, f32[32,128]{1,0:T(8,128)S(1)}, ...), condition=%wide.region_20.21_spmd, body=%wide.region_19.20_spmd.sunk | while | flops 34660548 | bytes 6842051 | solution.py:141
  596.6 4.9 fusion.210
  602.0 4.9 fusion.208
  611.9 4.9 fusion.210
  617.2 4.9 fusion.208
  627.2 4.9 fusion.210
  632.5 4.9 fusion.208
  641.0 4.2 collective-permute-done.25
  649.5 5.1 fusion.46
  654.7 11.7 %collective-permute-done.27 = f32[32,128]{1,0:T(8,128)S(1)} collective-permute-done((f32[32,128]{1,0:T(8,128)S(1)}, f32[32,128]{1,0:T(8,128)S(1)}, u32[]{:S(2)}, u32[]{:S(2)}) %collective-permute-start.27) | collective-permute-done | bytes 16416 | tf_op jit(solution)/shard_map/ppermute | solution.py:17
  667.0 85.1 %psum.47 = f32[]{:T(128)} all-reduce(f32[]{:T(128)} %get-tuple-element.336), channel_id=1, replica_groups=mesh['sky'=32,'gz'=8] {'sky','gz'}, use_global_device_ids=true, to_apply=%region_22.23 | all-reduce | flops 1 | bytes 8 | tf_op jit(solution)/shard_map/psum | solution.py:147
  (222 shorter events, 140.2 us)
Async XLA Ops:
  1.4 16.9 %collective-permute-start.4 = (f32[1,1,32,128]{3,2,1,0:T(8,128)S(1)}, f32[1,1,32,128]{3,2,1,0:T(8,128)S(1)}, u32[]{:S(2)}, u32[]{:S(2)}) collective-permute-start(f32[1,1,32,128]{3,2,1,0:T(8,128)S(1)} %select_multiply_fusion), channel_id=1, source_target_pairs={{0,8},{8,16},{16,24},{24,32},{32,40},{40,48},{48,56},{56,64},{64,7... | collective-permute-start | bytes 49160 | tf_op jit(solution)/shard_map/ppermute | solution.py:25
  5.9 12.4 %collective-permute-start.5 = (f32[1,1,32,128]{3,2,1,0:T(8,128)S(1)}, f32[1,1,32,128]{3,2,1,0:T(8,128)S(1)}, u32[]{:S(2)}, u32[]{:S(2)}) collective-permute-start(f32[1,1,32,128]{3,2,1,0:T(8,128)S(1)} %select_multiply_fusion), channel_id=1, source_target_pairs={{8,0},{16,8},{24,16},{32,24},{40,32},{48,40},{56,48},{64,56},{72,6... | collective-permute-start | bytes 49160 | tf_op jit(solution)/shard_map/ppermute | solution.py:28
  8.7 14.5 %collective-permute-start = (f32[1,1,32,3,128]{4,3,2,1,0:T(4,128)S(1)}, f32[1,1,32,3,128]{4,3,2,1,0:T(4,128)S(1)}, u32[]{:S(2)}, u32[]{:S(2)}) collective-permute-start(f32[1,1,32,3,128]{4,3,2,1,0:T(4,128)S(1)} %bitcast.383), channel_id=1, source_target_pairs={{0,8},{8,16},{16,24},{24,32},{32,40},{40,48},{48,56},{56,64},{64,7... | collective-permute-start | bytes 147464 | tf_op jit(solution)/shard_map/ppermute | solution.py:25
  12.4 10.8 %collective-permute-start.1 = (f32[1,1,32,3,128]{4,3,2,1,0:T(4,128)S(1)}, f32[1,1,32,3,128]{4,3,2,1,0:T(4,128)S(1)}, u32[]{:S(2)}, u32[]{:S(2)}) collective-permute-start(f32[1,1,32,3,128]{4,3,2,1,0:T(4,128)S(1)} %bitcast.384), channel_id=1, source_target_pairs={{8,0},{16,8},{24,16},{32,24},{40,32},{48,40},{56,48},{64,56},{72,6... | collective-permute-start | bytes 147464 | tf_op jit(solution)/shard_map/ppermute | solution.py:28
  18.3 12.0 %collective-permute-start.6 = (f32[3,1,32,128]{3,2,1,0:T(8,128)S(1)}, f32[3,1,32,128]{3,2,1,0:T(8,128)S(1)}, u32[]{:S(2)}, u32[]{:S(2)}) collective-permute-start(f32[3,1,32,128]{3,2,1,0:T(8,128)S(1)} %pad_maximum_fusion.5), channel_id=1, source_target_pairs={{0,1},{1,2},{2,3},{3,4},{4,5},{5,6},{6,7},{8,9},{9,10},{10,11},{11... | collective-permute-start | bytes 147464 | tf_op jit(solution)/shard_map/ppermute | solution.py:25
  21.9 8.5 %collective-permute-start.7 = (f32[3,1,32,128]{3,2,1,0:T(8,128)S(1)}, f32[3,1,32,128]{3,2,1,0:T(8,128)S(1)}, u32[]{:S(2)}, u32[]{:S(2)}) collective-permute-start(f32[3,1,32,128]{3,2,1,0:T(8,128)S(1)} %pad_maximum_fusion.5), channel_id=1, source_target_pairs={{1,0},{2,1},{3,2},{4,3},{5,4},{6,5},{7,6},{9,8},{10,9},{11,10},{12... | collective-permute-start | bytes 147464 | tf_op jit(solution)/shard_map/ppermute | solution.py:28
  23.3 7.9 %collective-permute-start.2 = (f32[3,1,32,3,128]{4,3,2,1,0:T(4,128)S(1)}, f32[3,1,32,3,128]{4,3,2,1,0:T(4,128)S(1)}, u32[]{:S(2)}, u32[]{:S(2)}) collective-permute-start(f32[3,1,32,3,128]{4,3,2,1,0:T(4,128)S(1)} %pad_maximum_fusion.1), channel_id=1, source_target_pairs={{0,1},{1,2},{2,3},{3,4},{4,5},{5,6},{6,7},{8,9},{9,10},{10,11},{11... | collective-permute-start | bytes 442376 | tf_op jit(solution)/shard_map/ppermute | solution.py:25
  27.4 7.8 %collective-permute-start.3 = (f32[3,1,32,3,128]{4,3,2,1,0:T(4,128)S(1)}, f32[3,1,32,3,128]{4,3,2,1,0:T(4,128)S(1)}, u32[]{:S(2)}, u32[]{:S(2)}) collective-permute-start(f32[3,1,32,3,128]{4,3,2,1,0:T(4,128)S(1)} %pad_maximum_fusion.1), channel_id=1, source_target_pairs={{1,0},{2,1},{3,2},{4,3},{5,4},{6,5},{7,6},{9,8},{10,9},{11,10},{12... | collective-permute-start | bytes 442376 | tf_op jit(solution)/shard_map/ppermute | solution.py:28
  122.9 11.0 %collective-permute-start.8 = (f32[3,32,128]{2,1,0:T(8,128)S(1)}, f32[3,32,128]{2,1,0:T(8,128)S(1)}, u32[]{:S(2)}, u32[]{:S(2)}) collective-permute-start(f32[3,32,128]{2,1,0:T(8,128)S(1)} %get-tuple-element.368), channel_id=1, source_target_pairs={{0,1},{1,2},{2,3},{3,4},{4,5},{5,6},{6,7},{8,9},{9,10},{10,11},{11... | collective-permute-start | bytes 147464 | tf_op jit(solution)/shard_map/ppermute | solution.py:17
  127.5 6.5 collective-permute-start.9
  128.8 27.3 %copy-start = (f32[1,1,32,128]{3,2,1,0:T(8,128)S(1)}, f32[1,1,32,128]{3,2,1,0:T(8,128)}, u32[]{:S(2)}) copy-start(f32[1,1,32,128]{3,2,1,0:T(8,128)} %param.16) | copy-start | bytes 49156
  128.8 27.3 %copy-start.1 = (f32[1,1,32,128]{3,2,1,0:T(8,128)S(1)}, f32[1,1,32,128]{3,2,1,0:T(8,128)}, u32[]{:S(2)}) copy-start(f32[1,1,32,128]{3,2,1,0:T(8,128)} %param.15) | copy-start | bytes 49156
  128.8 27.3 %copy-start.2 = (s32[1,1,32]{2,1,0:T(1,128)S(1)}, s32[1,1,32]{2,1,0:T(1,128)}, u32[]{:S(2)}) copy-start(s32[1,1,32]{2,1,0:T(1,128)} %param.18) | copy-start | bytes 388
  134.0 5.2 collective-permute-start.10
  135.9 20.1 %collective-permute-start.11 = (f32[32,128]{1,0:T(8,128)S(1)}, f32[32,128]{1,0:T(8,128)S(1)}, u32[]{:S(2)}, u32[]{:S(2)}) collective-permute-start(f32[32,128]{1,0:T(8,128)S(1)} %get-tuple-element.378), channel_id=1, source_target_pairs={{8,0},{16,8},{24,16},{32,24},{40,32},{48,40},{56,48},{64,56},{72,6... | collective-permute-start | bytes 49160 | tf_op jit(solution)/shard_map/ppermute | solution.py:17
  322.2 5.4 collective-permute-start.12
  325.7 5.1 collective-permute-start.13
  330.8 4.9 collective-permute-start.14
  334.4 4.8 collective-permute-start.15
  385.1 3.2 collective-permute-start.16
  387.1 5.5 collective-permute-start.17
  392.6 9.5 %collective-permute-start.18 = (f32[32,128]{1,0:T(8,128)S(1)}, f32[32,128]{1,0:T(8,128)S(1)}, u32[]{:S(2)}, u32[]{:S(2)}) collective-permute-start(f32[32,128]{1,0:T(8,128)S(1)} %get-tuple-element.375), channel_id=1, source_target_pairs={{0,8},{8,16},{16,24},{24,32},{32,40},{40,48},{48,56},{56,64},{64,7... | collective-permute-start | bytes 49160 | tf_op jit(solution)/shard_map/ppermute | solution.py:17
  394.5 18.2 %collective-permute-start.19 = (f32[32,128]{1,0:T(8,128)S(1)}, f32[32,128]{1,0:T(8,128)S(1)}, u32[]{:S(2)}, u32[]{:S(2)}) collective-permute-start(f32[32,128]{1,0:T(8,128)S(1)} %get-tuple-element.376), channel_id=1, source_target_pairs={{8,0},{16,8},{24,16},{32,24},{40,32},{48,40},{56,48},{64,56},{72,6... | collective-permute-start | bytes 49160 | tf_op jit(solution)/shard_map/ppermute | solution.py:17
  575.1 4.9 collective-permute-start.20
  578.1 5.1 collective-permute-start.21
  583.1 5.0 collective-permute-start.22
  586.8 4.8 collective-permute-start.23
  637.7 3.2 collective-permute-start.24
  639.7 5.5 collective-permute-start.25
  645.2 9.5 %collective-permute-start.26 = (f32[32,128]{1,0:T(8,128)S(1)}, f32[32,128]{1,0:T(8,128)S(1)}, u32[]{:S(2)}, u32[]{:S(2)}) collective-permute-start(f32[32,128]{1,0:T(8,128)S(1)} %get-tuple-element.373), channel_id=1, source_target_pairs={{0,8},{8,16},{16,24},{24,32},{32,40},{40,48},{48,56},{56,64},{64,7... | collective-permute-start | bytes 49160 | tf_op jit(solution)/shard_map/ppermute | solution.py:17
  647.1 19.2 %collective-permute-start.27 = (f32[32,128]{1,0:T(8,128)S(1)}, f32[32,128]{1,0:T(8,128)S(1)}, u32[]{:S(2)}, u32[]{:S(2)}) collective-permute-start(f32[32,128]{1,0:T(8,128)S(1)} %get-tuple-element.374), channel_id=1, source_target_pairs={{8,0},{16,8},{24,16},{32,24},{40,32},{48,40},{56,48},{64,56},{72,6... | collective-permute-start | bytes 49160 | tf_op jit(solution)/shard_map/ppermute | solution.py:17
where the time goes:
time: 757 us; the launch traced here: 754 us
  blocking collectives  406 us (54%)
  matrix products  142 us (19%)
  starting transfers between devices  67.7 us (9%)
  waiting for transfers between devices  65.7 us (9%)
  other arithmetic  35.2 us (5%)
  local copies, waits for them, and re-layouts  28.4 us (4%)
  between operations  8.13 us (1%)
    psum x3, blocking collectives, rz_total(): return lax.psum(jnp.sum(resid * precond_r), ('sky', 'gz'))  235 us
    psum x2, blocking collectives, local(): step_len = rz_now / lax.psum(jnp.sum(direction * image), ('sky', 'gz'))  171 us
    dot_general x21, matrix products, apply_tiles(): jnp.einsum('gab,gb->ga', tiles, vectors, precision=lax.Precision.HIGHEST)  104 us
    ppermute x12, waiting for transfers between devices, shifted(): return lax.ppermute(block, axis, route)  47.6 us
    dot_general x9, matrix products, apply_trans(): jnp.einsum('gab,ga->gb', tiles, vectors, precision=lax.Precision.HIGHEST)  31.1 us
    ppermute x8, starting transfers between devices, padded(): lax.ppermute(lax.slice_in_dim(block, block.shape[dim] - width, None, axis...  29.6 us
    ppermute x12, starting transfers between devices, shifted(): return lax.ppermute(block, axis, route)  25.2 us
    dynamic_update_slice x8, other arithmetic, local(): lax.map(cross_group, grouped).reshape(slot_count, blk_width, blk_width)  24.9 us
  transfers between devices with their start and end apart: 28, of which 11 were waited for; matrix products, arithmetic and copies ran while one was open for 3% of the time, Pallas kernels for 0%

commit v1 on v0

v1 whole, which is shorter than its diff:
```python
import functools
import jax
import jax.numpy as jnp
from jax import lax
from jax.experimental import pallas as pl
from jax.experimental.pallas import tpu as pltpu
from jax.sharding import PartitionSpec as P

ITERS = 3
BLOCKS = 32
WIDTH = 128
CODES = 9
OWN = 4
SUB = 8
INNER = 8

signal_amp = 0.25
bf16 = jnp.bfloat16
f32 = jnp.float32


def mm(left, right):
    return lax.dot_general(left, right, (((1,), (0,)), ((), ())), preferred_element_type=f32)


def mm_trans(left, right):
    return lax.dot_general(left, right, (((1,), (1,)), ((), ())), preferred_element_type=f32)


def split_two(values):
    high = values.astype(bf16)
    return high, (values - high.astype(f32)).astype(bf16)


def split_three(values):
    high = values.astype(bf16).astype(f32)
    rest = values - high
    mid = rest.astype(bf16).astype(f32)
    return high, mid, rest - mid


def body(
    slots,
    delta_ref, noise_ref, pos_ref, count_ref, pair_ref, spair_ref,
    field_ref, resid_ref,
    near_ref, cov_ref, msg_ref, first_ref, halo1_ref, halo2_ref, owed_ref, got_ref,
    gain_ref, pay_ref, self_ref, basis_ref, image_ref, onto_ref, from_ref,
    sum_ref, red1_ref, red2_ref, red3_ref,
    first_send, first_recv, halo_send, halo_recv, owed_send, owed_recv,
    red1_send, red1_recv, red2_send, red2_recv, red3_send, red3_recv,
):
    n_sky = lax.axis_size("sky")
    n_gz = lax.axis_size("gz")
    n_outer = n_sky // INNER
    me_s = lax.axis_index("sky")
    me_g = lax.axis_index("gz")
    outer = me_s // INNER
    inner = me_s % INNER

    def tile_at(code):
        return (
            (me_s + code // 3 - 1 + n_sky) % n_sky,
            (me_g + code % 3 - 1 + n_gz) % n_gz,
        )

    def gz_at(step):
        return (me_s, (me_g + step) % n_gz)

    def inner_at(step):
        return (outer * INNER + (inner + step) % INNER, me_g)

    def outer_at(step):
        return ((outer + step) % n_outer * INNER + inner, me_g)

    sides = [code for code in range(CODES) if code != OWN]
    partners = [tile_at(code) for code in sides]
    partners += [gz_at(step) for step in range(1, n_gz)]
    partners += [inner_at(step) for step in range(1, INNER)]
    partners += [outer_at(step) for step in range(1, n_outer)]
    barrier = pltpu.get_barrier_semaphore()
    for partner in partners:
        pl.semaphore_signal(
            barrier, inc=1, device_id=partner, device_id_type=pl.DeviceIdType.MESH
        )

    def remote(source, target, send, recv, device):
        return pltpu.make_async_remote_copy(
            src_ref=source, dst_ref=target, send_sem=send, recv_sem=recv,
            device_id=device, device_id_type=pl.DeviceIdType.MESH,
        )

    eye_b = lax.broadcasted_iota(jnp.int32, (BLOCKS, BLOCKS), 0) == lax.broadcasted_iota(
        jnp.int32, (BLOCKS, BLOCKS), 1
    )
    count = jnp.sum(
        jnp.where(eye_b, count_ref[...].astype(f32), 0.0), axis=1, keepdims=True
    )
    lanes = lax.broadcasted_iota(jnp.int32, (BLOCKS, WIDTH), 1).astype(f32)
    live = (lanes < count).astype(f32)
    noise = noise_ref[...]
    precond = 1.0 / (noise + signal_amp)
    right_side = live * delta_ref[...]
    image_ref[0] = right_side
    basis_ref[0] = precond * right_side

    msg_ref[0 : 3 * BLOCKS] = pos_ref[...]
    msg_ref[3 * BLOCKS :] = basis_ref[0]
    pl.semaphore_wait(barrier, len(partners))
    first = [
        remote(msg_ref, first_ref.at[8 - c], first_send.at[c], first_recv.at[8 - c], tile_at(c))
        for c in sides
    ]
    for copy in first:
        copy.start()
    first_ref[OWN] = msg_ref[...]

    codes = pair_ref[0:1, :]
    near_row = (codes >= 3).astype(jnp.int32) + (codes >= 6).astype(jnp.int32)
    row_s = me_s + near_row - 1
    row_g = me_g + (codes - 3 * near_row) - 1
    filled = codes < CODES
    inside = filled & (row_s >= 0) & (row_s < n_sky) & (row_g >= 0) & (row_g < n_gz)
    flat = jnp.minimum(codes, CODES - 1) * BLOCKS + pair_ref[1:2, :]
    target = pair_ref[2:3, :]
    weight = jnp.where(inside, signal_amp, 0.0)
    rows_b = lax.broadcasted_iota(jnp.int32, (BLOCKS, slots), 0)
    hits = rows_b == target
    onto = jnp.where(hits, weight, 0.0)
    onto_ref[:, :slots] = onto.astype(bf16)
    onto_ref[:, slots:] = onto.astype(bf16)
    named = jnp.sum(
        jnp.where(hits & filled, signal_amp, 0.0), axis=1, keepdims=True
    )
    rows_f = lax.broadcasted_iota(jnp.int32, (CODES * BLOCKS, slots), 0)
    backs = jnp.where(rows_f == flat, weight, 0.0)
    from_ref[:, :slots] = backs.astype(bf16)
    from_ref[:, slots:] = backs.astype(bf16)
    sourced = jnp.broadcast_to(
        jnp.sum(backs, axis=1, keepdims=True), (CODES * BLOCKS, WIDTH)
    )
    for c in range(CODES):
        owed_ref[0, c, BLOCKS:] = sourced[c * BLOCKS : (c + 1) * BLOCKS]

    mid_x = (2 * me_s + 1).astype(f32)
    mid_z = (4 * me_g + 2).astype(f32)
    sub = lax.broadcasted_iota(jnp.int32, (SUB, WIDTH), 0)

    def features(code, block, swap):
        x = first_ref[code, pl.ds(block, 1), :] - mid_x
        y = first_ref[code, pl.ds(BLOCKS + block, 1), :] - 1.0
        z = first_ref[code, pl.ds(2 * BLOCKS + block, 1), :] - mid_z
        size = -0.5 * (x * x + y * y + z * z)
        tile = jnp.where(sub == 0, x, 0.0)
        tile = jnp.where(sub == 1, y, tile)
        tile = jnp.where(sub == 2, z, tile)
        tile = jnp.where(sub == (3 if swap else 4), size, tile)
        return jnp.where(sub == (4 if swap else 3), 1.0, tile)

    blank = jnp.zeros((WIDTH - 6 * SUB, WIDTH), f32)

    def near_step(block, _):
        h, m, l = split_three(features(OWN, block, True))
        stack = jnp.concatenate([h, h, m, m, h, l, blank], axis=0)
        near_ref[block] = jnp.transpose(stack).astype(bf16)
        return 0

    lax.fori_loop(0, BLOCKS, near_step, 0)

    def make_tile(slot, block, code, source):
        h, m, l = split_three(features(code, source, False))
        stack = jnp.concatenate([h, m, h, m, l, h, blank], axis=0).astype(bf16)
        values = jnp.exp(mm(near_ref[block], stack))
        high, low = split_two(values)
        cov_ref[slot, 0:WIDTH] = high
        cov_ref[slot, WIDTH:] = low

    def self_tile(step, _):
        for k in range(4):
            block = step * 4 + k
            make_tile(slots + block, block, OWN, block)
        return 0

    lax.fori_loop(0, BLOCKS // 4, self_tile, 0)
    for copy in first:
        copy.wait_recv()

    def pair_tile(step, _):
        for k in range(4):
            slot = step * 4 + k
            code = jnp.minimum(spair_ref[0, slot], CODES - 1)
            make_tile(slot, spair_ref[2, slot], code, spair_ref[1, slot])
        return 0

    lax.fori_loop(0, slots // 4, pair_tile, 0)

    def packed(rows):
        high, low = split_two(rows)
        return jnp.concatenate([high, low], axis=0)

    def doubled(values):
        high, low = split_two(values)
        return jnp.concatenate([high, low], axis=0)

    in_flight = []
    own_weight = None
    for it in range(ITERS):
        vector = basis_ref[it]
        if it == 0:
            arriving = []
            far_at = lambda code, block: first_ref[code, pl.ds(3 * BLOCKS + block, 1), :]
        else:
            halo_ref = (halo1_ref, halo2_ref)[it - 1]
            arriving = [
                remote(
                    basis_ref.at[it], halo_ref.at[8 - c],
                    halo_send.at[it - 1, c], halo_recv.at[it - 1, 8 - c], tile_at(c),
                )
                for c in sides
            ]
            for copy in arriving:
                copy.start()
            halo_ref[OWN] = vector
            far_at = functools.partial(
                lambda ref, code, block: ref[code, pl.ds(block, 1), :], halo_ref
            )

        def pay_step(step, _):
            rows = jnp.zeros((SUB, WIDTH), f32)
            for k in range(SUB):
                block = spair_ref[2, step * SUB + k]
                rows = jnp.where(sub == k, basis_ref[it, pl.ds(block, 1), :], rows)
            left = packed(rows)
            left = jnp.concatenate([left, left], axis=1)
            total = jnp.zeros((SUB, WIDTH), f32)
            for k in range(SUB):
                out = mm(left, cov_ref[step * SUB + k])
                total = jnp.where(sub == k, out[:SUB] + out[SUB:], total)
            pay_ref[pl.ds(step * SUB, SUB), :] = total
            return 0

        lax.fori_loop(0, slots // SUB, pay_step, 0)
        owed = mm(from_ref[...], doubled(pay_ref[...]))
        for c in range(CODES):
            owed_ref[it, c, 0:BLOCKS] = owed[c * BLOCKS : (c + 1) * BLOCKS]
        extent = 2 * BLOCKS if it == 0 else BLOCKS
        returns = [
            remote(
                owed_ref.at[it, c, pl.ds(0, extent)], got_ref.at[it, 8 - c, pl.ds(0, extent)],
                owed_send.at[it, c], owed_recv.at[it, 8 - c], tile_at(c),
            )
            for c in sides
        ]
        for copy in returns:
            copy.start()

        def self_step(step, _):
            left = packed(basis_ref[it, pl.ds(step * SUB, SUB), :])
            left = jnp.concatenate([left, left], axis=1)
            total = jnp.zeros((SUB, WIDTH), f32)
            for k in range(SUB):
                out = mm(left, cov_ref[slots + step * SUB + k])
                total = jnp.where(sub == k, out[:SUB] + out[SUB:], total)
            self_ref[pl.ds(step * SUB, SUB), :] = total
            return 0

        lax.fori_loop(0, BLOCKS // SUB, self_step, 0)
        for copy in arriving:
            copy.wait_recv()

        def gain_step(step, _):
            rows = jnp.zeros((SUB, WIDTH), f32)
            for k in range(SUB):
                slot = step * SUB + k
                code = jnp.minimum(spair_ref[0, slot], CODES - 1)
                rows = jnp.where(sub == k, far_at(code, spair_ref[1, slot]), rows)
            left = packed(rows)
            total = jnp.zeros((SUB, WIDTH), f32)
            for k in range(SUB):
                out = mm_trans(left, cov_ref[step * SUB + k])
                out = out[:SUB] + out[SUB:]
                total = jnp.where(sub == k, out[:, :WIDTH] + out[:, WIDTH:], total)
            gain_ref[pl.ds(step * SUB, SUB), :] = total
            return 0

        lax.fori_loop(0, slots // SUB, gain_step, 0)
        totals = mm(onto_ref[...], doubled(gain_ref[...])) + owed_ref[it, OWN, 0:BLOCKS]
        for copy in returns:
            copy.wait_recv()
        for c in sides:
            totals = totals + got_ref[it, c, 0:BLOCKS]
        if it == 0:
            own_weight = owed_ref[0, OWN, BLOCKS:] + (signal_amp + named)
            for c in sides:
                own_weight = own_weight + got_ref[0, c, BLOCKS:]
        totals = totals + own_weight * self_ref[...]
        image = live * totals + noise * vector
        image_ref[it + 1] = image
        basis_ref[it + 1] = precond * image
        in_flight += arriving + returns

    moments = jnp.zeros((SUB, WIDTH), f32)
    for m in range(2 * ITERS + 1):
        product = basis_ref[m // 2] * image_ref[m - m // 2]
        moments = jnp.where(sub == m, jnp.sum(product, axis=0, keepdims=True), moments)
    stages = (
        (gz_at, n_gz, red1_ref, red1_send, red1_recv),
        (inner_at, INNER, red2_ref, red2_send, red2_recv),
        (outer_at, n_outer, red3_ref, red3_send, red3_recv),
    )
    for stage, (device_at, members, into, send, recv) in enumerate(stages):
        sum_ref[stage] = moments
        copies = [
            remote(
                sum_ref.at[stage], into.at[step - 1], send.at[step - 1], recv.at[step - 1],
                device_at(step),
            )
            for step in range(1, members)
        ]
        for copy in copies:
            copy.start()
        for step, copy in enumerate(copies):
            copy.wait_recv()
            moments = moments + into[step]
        in_flight += copies
    total = jnp.sum(moments, axis=1, keepdims=True)
    mu = [total[m : m + 1] for m in range(2 * ITERS + 1)]

    def inner_product(left, right):
        value = None
        for i, a in enumerate(left):
            for j, b in enumerate(right):
                if a is not None and b is not None:
                    term = a * b * mu[i + j]
                    value = term if value is None else value + term
        return value

    def plus(left, scale, right):
        if right is None:
            return left
        return scale * right if left is None else left + scale * right

    one = jnp.ones((1, 1), f32)
    resid = [one, None, None, None]
    direct = [one, None, None, None]
    field = [None, None, None, None]
    rz = mu[0]
    for it in range(ITERS):
        moved = [None] + direct[:-1]
        alpha = rz / inner_product(direct, moved)
        field = [plus(a, alpha, b) for a, b in zip(field, direct)]
        resid = [plus(a, -alpha, b) for a, b in zip(resid, moved)]
        if it + 1 < ITERS:
            new = inner_product(resid, resid)
            beta = new / rz
            direct = [plus(a, beta, b) for a, b in zip(resid, direct)]
            rz = new
    out_field = field[0] * basis_ref[0]
    for i in range(1, ITERS):
        out_field = out_field + field[i] * basis_ref[i]
    out_resid = image_ref[0]
    for i in range(1, ITERS + 1):
        out_resid = out_resid + resid[i] * image_ref[i]
    field_ref[...] = out_field
    resid_ref[...] = out_resid
    for copy in first + in_flight:
        copy.wait_send()


def local(delta_flux, noise_var, pixel_pos, pixel_count, pair_list):
    slots = pair_list.shape[3]
    n_sky = lax.axis_size("sky")
    n_gz = lax.axis_size("gz")
    n_outer = n_sky // INNER
    pairs = pair_list[0, 0]
    vmem = pl.BlockSpec(memory_space=pltpu.VMEM)
    smem = pl.BlockSpec(memory_space=pltpu.SMEM)
    shape = jax.ShapeDtypeStruct((BLOCKS, WIDTH), f32)
    dma = pltpu.SemaphoreType.DMA
    field, resid = pl.pallas_call(
        functools.partial(body, slots),
        out_shape=(shape, shape),
        in_specs=[vmem, vmem, vmem, vmem, vmem, smem],
        out_specs=(vmem, vmem),
        scratch_shapes=[
            pltpu.VMEM((BLOCKS, WIDTH, WIDTH), bf16),
            pltpu.VMEM((slots + BLOCKS, 2 * WIDTH, WIDTH), bf16),
            pltpu.VMEM((4 * BLOCKS, WIDTH), f32),
            pltpu.VMEM((CODES, 4 * BLOCKS, WIDTH), f32),
            pltpu.VMEM((CODES, BLOCKS, WIDTH), f32),
            pltpu.VMEM((CODES, BLOCKS, WIDTH), f32),
            pltpu.VMEM((ITERS, CODES, 2 * BLOCKS, WIDTH), f32),
            pltpu.VMEM((ITERS, CODES, 2 * BLOCKS, WIDTH), f32),
            pltpu.VMEM((slots, WIDTH), f32),
            pltpu.VMEM((slots, WIDTH), f32),
            pltpu.VMEM((BLOCKS, WIDTH), f32),
            pltpu.VMEM((ITERS + 1, BLOCKS, WIDTH), f32),
            pltpu.VMEM((ITERS + 1, BLOCKS, WIDTH), f32),
            pltpu.VMEM((BLOCKS, 2 * slots), bf16),
            pltpu.VMEM((CODES * BLOCKS, 2 * slots), bf16),
            pltpu.VMEM((3, SUB, WIDTH), f32),
            pltpu.VMEM((n_gz - 1, SUB, WIDTH), f32),
            pltpu.VMEM((INNER - 1, SUB, WIDTH), f32),
            pltpu.VMEM((n_outer - 1, SUB, WIDTH), f32),
            dma((CODES,)), dma((CODES,)),
            dma((ITERS - 1, CODES)), dma((ITERS - 1, CODES)),
            dma((ITERS, CODES)), dma((ITERS, CODES)),
            dma((n_gz - 1,)), dma((n_gz - 1,)),
            dma((INNER - 1,)), dma((INNER - 1,)),
            dma((n_outer - 1,)), dma((n_outer - 1,)),
        ],
        compiler_params=pltpu.CompilerParams(
            collective_id=0, has_side_effects=True, vmem_limit_bytes=40 * 1024 * 1024
        ),
    )(
        delta_flux[0, 0],
        noise_var[0, 0],
        pixel_pos.reshape(3 * BLOCKS, WIDTH),
        pixel_count.reshape(1, BLOCKS),
        pairs,
        pairs,
    )
    return field[None, None], resid[None, None]


def solution(mesh):
    placed = (
        P("sky", "gz", None, None),
        P("sky", "gz", None, None),
        P("sky", "gz", None, None, None),
        P("sky", "gz", None),
        P("sky", "gz", None, None),
    )
    return jax.shard_map(
        local,
        mesh=mesh,
        in_specs=placed,
        out_specs=(P("sky", "gz", None, None), P("sky", "gz", None, None)),
        check_vma=False,
    )
```

time: 757 us -> 68.2 us (0.09)
  blocking collectives: 406 us -> 0 us
  matrix products: 142 us -> 0 us
  starting transfers between devices: 67.7 us -> 0 us
  waiting for transfers between devices: 65.7 us -> 0 us
  Pallas kernels: 0 us -> 62.5 us
  other arithmetic: 35.2 us -> 0 us
  local copies, waits for them, and re-layouts: 28.4 us -> 4.77 us
    psum x5 -> x0, blocking collectives: 406 us -> none  [the longest x3 235 us: rz_total(): return lax.psum(jnp.sum(resid * precond_r), ('sky', 'gz'))]
    dot_general x49 -> x0, matrix products: 142 us -> none  [the longest x21 104 us: apply_tiles(): jnp.einsum('gab,gb->ga', tiles, vectors, precision=lax.Precision.HIGHEST)]
    ppermute x28 -> x0, starting transfers between devices: 67.7 us -> none  [the longest x8 29.6 us: padded(): lax.ppermute(lax.slice_in_dim(block, block.shape[dim] - width, None, axis...]
    ppermute x28 -> x0, waiting for transfers between devices: 65.7 us -> none  [the longest x12 47.6 us: shifted(): return lax.ppermute(block, axis, route)]
    pallas_call x0 -> x1, Pallas kernels: none -> 62.5 us  [local(): pl.pallas_call(functools.partial(body, slots), out_shape=(shape, shape),...]
    dynamic_update_slice x8 -> x0, other arithmetic: 24.9 us -> none  [local(): lax.map(cross_group, grouped).reshape(slot_count, blk_width, blk_width)]
    gather x30 -> x0, local copies, waits for them, and re-layouts: 17.7 us -> none  [the longest x9 5.22 us: own_step(): far_vec = halo_vec[flat_src]]
    another operation x9 -> x0, local copies, waits for them, and re-layouts: 8.69 us -> none
  transfers between devices with their start and end apart: 28 -> 0, of which waited for: 11 -> 0; matrix products, arithmetic and copies ran while one was open for 3% -> 0% of each run, Pallas kernels for 0% -> 0%
where the time goes in v1:
time: 68.2 us; the launch traced here: 68 us
  Pallas kernels  62.5 us (92%)
  local copies, waits for them, and re-layouts  4.77 us (7%)
    pallas_call x1, Pallas kernels, local(): pl.pallas_call(functools.partial(body, slots), out_shape=(shape, shape),...  62.5 us
    unnamed x13, local copies, waits for them, and re-layouts  4.77 us

profile of v1, /device:TPU:1, one launch (start us, length us, event | category | flops | bytes accessed | tf_op | source)
XLA Modules:
  0.0 68.0 jit_solution(15941083158483318675)
XLA Ops:
  0.6 0.0 copy-start.4
  0.6 0.7 copy-done.4
  1.3 0.0 copy-start.3
  1.3 0.7 copy-done.3
  2.0 0.0 copy-start
  2.0 0.8 %copy-done = f32[1,1,3,32,128]{4,3,2,1,0:T(8,128)S(1)} copy-done((f32[1,1,3,32,128]{4,3,2,1,0:T(8,128)S(1)}, f32[1,1,3,32,128]{4,3,2,1,0:T(8,128)}, u32[]{:S(2)}) %copy-start) | copy-done | bytes 49176
  2.8 0.0 copy-start.1
  2.8 0.7 %copy-done.1 = f32[1,1,32,128]{3,2,1,0:T(8,128)S(1)} copy-done((f32[1,1,32,128]{3,2,1,0:T(8,128)S(1)}, f32[1,1,32,128]{3,2,1,0:T(8,128)}, u32[]{:S(2)}) %copy-start.1) | copy-done | bytes 16408
  3.5 0.0 copy-start.2
  3.5 0.7 %copy-done.2 = f32[1,1,32,128]{3,2,1,0:T(8,128)S(1)} copy-done((f32[1,1,32,128]{3,2,1,0:T(8,128)S(1)}, f32[1,1,32,128]{3,2,1,0:T(8,128)}, u32[]{:S(2)}) %copy-start.2) | copy-done | bytes 16408
  4.2 62.5 %shard_map.68 = (f32[32,128]{1,0:T(8,128)S(1)}, f32[32,128]{1,0:T(8,128)S(1)}) custom-call(f32[32,128]{1,0:T(8,128)S(1)} %bitcast.14, f32[32,128]{1,0:T(8,128)S(1)} %bitcast.15, f32[96,128]{1,0:T(8,128)S(1)} %bitcast.9, s32[1,32]{1,0:T(1,128)S(1)} %bitcast.16, s32[3,128]{1,0:T(4,128)S(1)} %bitcast.10, s32[3,128]{1,0:T(4,128)S(1)} %bitcast.11), custom_call_target="tpu_custom_call" | custom-call | tf_op jit(solution)/shard_map/pallas_call | solution.py:379
  66.7 0.6 copy.12
  67.4 0.6 copy.13
  (1 shorter events, 0.0 us)
Async XLA Ops:
  0.6 0.7 %copy-start.4 = (s32[1,1,3,128]{3,1,2,0:T(1,128)S(1)}, s32[1,1,3,128]{3,1,2,0:T(1,128)}, u32[]{:S(2)}) copy-start(s32[1,1,3,128]{3,1,2,0:T(1,128)} %param.9) | copy-start | bytes 4612
  1.3 0.7 copy-start.3
  2.0 0.8 %copy-start = (f32[1,1,3,32,128]{4,3,2,1,0:T(8,128)S(1)}, f32[1,1,3,32,128]{4,3,2,1,0:T(8,128)}, u32[]{:S(2)}) copy-start(f32[1,1,3,32,128]{4,3,2,1,0:T(8,128)} %param.7) | copy-start | bytes 147460
  2.8 0.7 %copy-start.1 = (f32[1,1,32,128]{3,2,1,0:T(8,128)S(1)}, f32[1,1,32,128]{3,2,1,0:T(8,128)}, u32[]{:S(2)}) copy-start(f32[1,1,32,128]{3,2,1,0:T(8,128)} %param.5) | copy-start | bytes 49156
  3.5 0.7 %copy-start.2 = (f32[1,1,32,128]{3,2,1,0:T(8,128)S(1)}, f32[1,1,32,128]{3,2,1,0:T(8,128)}, u32[]{:S(2)}) copy-start(f32[1,1,32,128]{3,2,1,0:T(8,128)} %param.6) | copy-start | bytes 49156

commit v2 on v1

--- a/solution.py
+++ b/solution.py
@@ -1,4 +1,5 @@
 import functools
+import math
 import jax
 import jax.numpy as jnp
 from jax import lax
@@ -41,12 +42,13 @@
 
 def body(
     slots,
+    delta_in, noise_in, pos_in, count_in, pair_in,
+    field_ref, resid_ref,
     delta_ref, noise_ref, pos_ref, count_ref, pair_ref, spair_ref,
-    field_ref, resid_ref,
-    near_ref, cov_ref, msg_ref, first_ref, halo1_ref, halo2_ref, owed_ref, got_ref,
+    near_ref, cov_ref, first_ref, halo0_ref, halo1_ref, halo2_ref, owed_ref, got_ref,
     gain_ref, pay_ref, self_ref, basis_ref, image_ref, onto_ref, from_ref,
     sum_ref, red1_ref, red2_ref, red3_ref,
-    first_send, first_recv, halo_send, halo_recv, owed_send, owed_recv,
+    load_sem, first_send, first_recv, halo_send, halo_recv, owed_send, owed_recv,
     red1_send, red1_recv, red2_send, red2_recv, red3_send, red3_recv,
 ):
     n_sky = lax.axis_size("sky")
@@ -77,6 +79,21 @@
     partners += [gz_at(step) for step in range(1, n_gz)]
     partners += [inner_at(step) for step in range(1, INNER)]
     partners += [outer_at(step) for step in range(1, n_outer)]
+    loads = [
+        pltpu.make_async_copy(source, into, load_sem.at[i])
+        for i, (source, into) in enumerate(
+            (
+                (pos_in.at[0, 0], pos_ref),
+                (pair_in.at[0], pair_ref),
+                (pair_in.at[0], spair_ref),
+                (count_in.at[0], count_ref),
+                (noise_in.at[0, 0], noise_ref),
+                (delta_in.at[0, 0], delta_ref),
+            )
+        )
+    ]
+    for copy in loads:
+        copy.start()
     barrier = pltpu.get_barrier_semaphore()
     for partner in partners:
         pl.semaphore_signal(
@@ -88,6 +105,26 @@
             src_ref=source, dst_ref=target, send_sem=send, recv_sem=recv,
             device_id=device, device_id_type=pl.DeviceIdType.MESH,
         )
+
+    for copy in loads:
+        copy.wait()
+    pl.semaphore_wait(barrier, len(partners))
+    first = [
+        remote(pos_ref, first_ref.at[8 - c], first_send.at[c], first_recv.at[8 - c], tile_at(c))
+        for c in sides
+    ]
+    for copy in first:
+        copy.start()
+    first_ref[OWN] = pos_ref[...]
+
+    def halo_copies(it, into):
+        return [
+            remote(
+                basis_ref.at[it], into.at[8 - c],
+                halo_send.at[it, c], halo_recv.at[it, 8 - c], tile_at(c),
+            )
+            for c in sides
+        ]
 
     eye_b = lax.broadcasted_iota(jnp.int32, (BLOCKS, BLOCKS), 0) == lax.broadcasted_iota(
         jnp.int32, (BLOCKS, BLOCKS), 1
@@ -103,25 +140,20 @@
     image_ref[0] = right_side
     basis_ref[0] = precond * right_side
 
-    msg_ref[0 : 3 * BLOCKS] = pos_ref[...]
-    msg_ref[3 * BLOCKS :] = basis_ref[0]
-    pl.semaphore_wait(barrier, len(partners))
-    first = [
-        remote(msg_ref, first_ref.at[8 - c], first_send.at[c], first_recv.at[8 - c], tile_at(c))
-        for c in sides
-    ]
-    for copy in first:
+    halo_refs = (halo0_ref, halo1_ref, halo2_ref)
+    arriving = halo_copies(0, halo0_ref)
+    for copy in arriving:
         copy.start()
-    first_ref[OWN] = msg_ref[...]
-
-    codes = pair_ref[0:1, :]
+    halo0_ref[OWN] = basis_ref[0]
+
+    codes = pair_ref[0]
     near_row = (codes >= 3).astype(jnp.int32) + (codes >= 6).astype(jnp.int32)
     row_s = me_s + near_row - 1
     row_g = me_g + (codes - 3 * near_row) - 1
     filled = codes < CODES
     inside = filled & (row_s >= 0) & (row_s < n_sky) & (row_g >= 0) & (row_g < n_gz)
-    flat = jnp.minimum(codes, CODES - 1) * BLOCKS + pair_ref[1:2, :]
-    target = pair_ref[2:3, :]
+    flat = jnp.minimum(codes, CODES - 1) * BLOCKS + pair_ref[1]
+    target = pair_ref[2]
     weight = jnp.where(inside, signal_amp, 0.0)
     rows_b = lax.broadcasted_iota(jnp.int32, (BLOCKS, slots), 0)
     hits = rows_b == target
@@ -143,12 +175,13 @@
 
     mid_x = (2 * me_s + 1).astype(f32)
     mid_z = (4 * me_g + 2).astype(f32)
+    scale = math.sqrt(math.log2(math.e))
     sub = lax.broadcasted_iota(jnp.int32, (SUB, WIDTH), 0)
 
     def features(code, block, swap):
-        x = first_ref[code, pl.ds(block, 1), :] - mid_x
-        y = first_ref[code, pl.ds(BLOCKS + block, 1), :] - 1.0
-        z = first_ref[code, pl.ds(2 * BLOCKS + block, 1), :] - mid_z
+        x = (first_ref[code, 0, pl.ds(block, 1), :] - mid_x) * scale
+        y = (first_ref[code, 1, pl.ds(block, 1), :] - 1.0) * scale
+        z = (first_ref[code, 2, pl.ds(block, 1), :] - mid_z) * scale
         size = -0.5 * (x * x + y * y + z * z)
         tile = jnp.where(sub == 0, x, 0.0)
         tile = jnp.where(sub == 1, y, tile)
@@ -169,7 +202,7 @@
     def make_tile(slot, block, code, source):
         h, m, l = split_three(features(code, source, False))
         stack = jnp.concatenate([h, m, h, m, l, h, blank], axis=0).astype(bf16)
-        values = jnp.exp(mm(near_ref[block], stack))
+        values = jnp.exp2(mm(near_ref[block], stack))
         high, low = split_two(values)
         cov_ref[slot, 0:WIDTH] = high
         cov_ref[slot, WIDTH:] = low
@@ -184,15 +217,6 @@
     for copy in first:
         copy.wait_recv()
 
-    def pair_tile(step, _):
-        for k in range(4):
-            slot = step * 4 + k
-            code = jnp.minimum(spair_ref[0, slot], CODES - 1)
-            make_tile(slot, spair_ref[2, slot], code, spair_ref[1, slot])
-        return 0
-
-    lax.fori_loop(0, slots // 4, pair_tile, 0)
-
     def packed(rows):
         high, low = split_two(rows)
         return jnp.concatenate([high, low], axis=0)
@@ -205,29 +229,22 @@
     own_weight = None
     for it in range(ITERS):
         vector = basis_ref[it]
-        if it == 0:
-            arriving = []
-            far_at = lambda code, block: first_ref[code, pl.ds(3 * BLOCKS + block, 1), :]
-        else:
-            halo_ref = (halo1_ref, halo2_ref)[it - 1]
-            arriving = [
-                remote(
-                    basis_ref.at[it], halo_ref.at[8 - c],
-                    halo_send.at[it - 1, c], halo_recv.at[it - 1, 8 - c], tile_at(c),
-                )
-                for c in sides
-            ]
+        halo_ref = halo_refs[it]
+        if it > 0:
+            arriving = halo_copies(it, halo_ref)
             for copy in arriving:
                 copy.start()
             halo_ref[OWN] = vector
-            far_at = functools.partial(
-                lambda ref, code, block: ref[code, pl.ds(block, 1), :], halo_ref
-            )
 
         def pay_step(step, _):
+            if it == 0:
+                for k in range(SUB):
+                    slot = step * SUB + k
+                    code = jnp.minimum(spair_ref[0, 0, slot], CODES - 1)
+                    make_tile(slot, spair_ref[2, 0, slot], code, spair_ref[1, 0, slot])
             rows = jnp.zeros((SUB, WIDTH), f32)
             for k in range(SUB):
-                block = spair_ref[2, step * SUB + k]
+                block = spair_ref[2, 0, step * SUB + k]
                 rows = jnp.where(sub == k, basis_ref[it, pl.ds(block, 1), :], rows)
             left = packed(rows)
             left = jnp.concatenate([left, left], axis=1)
@@ -271,8 +288,8 @@
             rows = jnp.zeros((SUB, WIDTH), f32)
             for k in range(SUB):
                 slot = step * SUB + k
-                code = jnp.minimum(spair_ref[0, slot], CODES - 1)
-                rows = jnp.where(sub == k, far_at(code, spair_ref[1, slot]), rows)
+                code = jnp.minimum(spair_ref[0, 0, slot], CODES - 1)
+                rows = jnp.where(sub == k, halo_ref[code, pl.ds(spair_ref[1, 0, slot], 1), :], rows)
             left = packed(rows)
             total = jnp.zeros((SUB, WIDTH), f32)
             for k in range(SUB):
@@ -371,21 +388,26 @@
     n_sky = lax.axis_size("sky")
     n_gz = lax.axis_size("gz")
     n_outer = n_sky // INNER
-    pairs = pair_list[0, 0]
     vmem = pl.BlockSpec(memory_space=pltpu.VMEM)
-    smem = pl.BlockSpec(memory_space=pltpu.SMEM)
+    hbm = pl.BlockSpec(memory_space=pltpu.HBM)
     shape = jax.ShapeDtypeStruct((BLOCKS, WIDTH), f32)
     dma = pltpu.SemaphoreType.DMA
     field, resid = pl.pallas_call(
         functools.partial(body, slots),
         out_shape=(shape, shape),
-        in_specs=[vmem, vmem, vmem, vmem, vmem, smem],
+        in_specs=[hbm] * 5,
         out_specs=(vmem, vmem),
         scratch_shapes=[
+            pltpu.VMEM((BLOCKS, WIDTH), f32),
+            pltpu.VMEM((BLOCKS, WIDTH), f32),
+            pltpu.VMEM((3, BLOCKS, WIDTH), f32),
+            pltpu.VMEM((1, BLOCKS), jnp.int32),
+            pltpu.VMEM((3, 1, slots), jnp.int32),
+            pltpu.SMEM((3, 1, slots), jnp.int32),
             pltpu.VMEM((BLOCKS, WIDTH, WIDTH), bf16),
             pltpu.VMEM((slots + BLOCKS, 2 * WIDTH, WIDTH), bf16),
-            pltpu.VMEM((4 * BLOCKS, WIDTH), f32),
-            pltpu.VMEM((CODES, 4 * BLOCKS, WIDTH), f32),
+            pltpu.VMEM((CODES, 3, BLOCKS, WIDTH), f32),
+            pltpu.VMEM((CODES, BLOCKS, WIDTH), f32),
             pltpu.VMEM((CODES, BLOCKS, WIDTH), f32),
             pltpu.VMEM((CODES, BLOCKS, WIDTH), f32),
             pltpu.VMEM((ITERS, CODES, 2 * BLOCKS, WIDTH), f32),
@@ -401,8 +423,8 @@
             pltpu.VMEM((n_gz - 1, SUB, WIDTH), f32),
             pltpu.VMEM((INNER - 1, SUB, WIDTH), f32),
             pltpu.VMEM((n_outer - 1, SUB, WIDTH), f32),
-            dma((CODES,)), dma((CODES,)),
-            dma((ITERS - 1, CODES)), dma((ITERS - 1, CODES)),
+            dma((6,)), dma((CODES,)), dma((CODES,)),
+            dma((ITERS, CODES)), dma((ITERS, CODES)),
             dma((ITERS, CODES)), dma((ITERS, CODES)),
             dma((n_gz - 1,)), dma((n_gz - 1,)),
             dma((INNER - 1,)), dma((INNER - 1,)),
@@ -412,12 +434,12 @@
             collective_id=0, has_side_effects=True, vmem_limit_bytes=40 * 1024 * 1024
         ),
     )(
-        delta_flux[0, 0],
-        noise_var[0, 0],
-        pixel_pos.reshape(3 * BLOCKS, WIDTH),
-        pixel_count.reshape(1, BLOCKS),
-        pairs,
-        pairs,
+        *(
+            pltpu.with_memory_space_constraint(value, pltpu.HBM)
+            for value in (
+                delta_flux, noise_var, pixel_pos, pixel_count, jnp.transpose(pair_list, (0, 2, 1, 3))
+            )
+        )
     )
     return field[None, None], resid[None, None]
 

time: 68.2 us -> 60.7 us (0.89)
  Pallas kernels: 62.5 us -> 58.7 us
  local copies, waits for them, and re-layouts: 4.77 us -> 1.21 us
    pallas_call x1, Pallas kernels: 62.5 us -> 58.7 us  [local(): pl.pallas_call(functools.partial(body, slots), out_shape=(shape, shape),...]
    unnamed x13 -> x2, local copies, waits for them, and re-layouts: 4.77 us -> 1.21 us
where the time goes in v2:
time: 60.7 us; the launch traced here: 60.6 us
  Pallas kernels  58.7 us (97%)
  local copies, waits for them, and re-layouts  1.21 us (2%)
  between operations  0.64 us (1%)
    pallas_call x1, Pallas kernels, local(): pl.pallas_call(functools.partial(body, slots), out_shape=(shape, shape),...  58.7 us

profile of v2, /device:TPU:1, one launch (start us, length us, event | category | flops | bytes accessed | tf_op | source)
XLA Modules:
  0.0 60.6 jit_solution(9100086034867625886)
XLA Ops:
  0.6 58.7 %shard_map.68 = (f32[32,128]{1,0:T(8,128)S(1)}, f32[32,128]{1,0:T(8,128)S(1)}) custom-call(f32[1,1,32,128]{3,2,1,0:T(8,128)} %delta_in.1, f32[1,1,32,128]{3,2,1,0:T(8,128)} %noise_in.1, f32[1,1,3,32,128]{4,3,2,1,0:T(8,128)} %pos_in.1, s32[1,1,32]{2,1,0:T(1,128)} %count_in.1, s32[1,3,1,128]{3,2,1,0:T(1,128)} %bitcast.5), custom_call_target="tpu_custom_call" | custom-call | tf_op jit(solution)/shard_map/pallas_call | solution.py:395
  59.3 0.6 %copy.9 = f32[1,1,32,128]{3,2,1,0:T(8,128)} copy(f32[1,1,32,128]{3,2,1,0:T(8,128)S(1)} %bitcast.4) | data formatting | bytes 32768
  60.0 0.6 copy.10

commit v3 on v2

--- a/solution.py
+++ b/solution.py
@@ -14,6 +14,7 @@
 OWN = 4
 SUB = 8
 INNER = 8
+BY_UNIT = (1, 4, 7)
 
 signal_amp = 0.25
 bf16 = jnp.bfloat16
@@ -45,8 +46,8 @@
     delta_in, noise_in, pos_in, count_in, pair_in,
     field_ref, resid_ref,
     delta_ref, noise_ref, pos_ref, count_ref, pair_ref, spair_ref,
-    near_ref, cov_ref, first_ref, halo0_ref, halo1_ref, halo2_ref, owed_ref, got_ref,
-    gain_ref, pay_ref, self_ref, basis_ref, image_ref, onto_ref, from_ref,
+    near_ref, cov_ref, column_ref, first_ref, halo0_ref, halo1_ref, halo2_ref, owed_ref, got_ref,
+    pay_ref, self_ref, basis_ref, image_ref, onto_ref, from_ref,
     sum_ref, red1_ref, red2_ref, red3_ref,
     load_sem, first_send, first_recv, halo_send, halo_recv, owed_send, owed_recv,
     red1_send, red1_recv, red2_send, red2_recv, red3_send, red3_recv,
@@ -202,10 +203,7 @@
     def make_tile(slot, block, code, source):
         h, m, l = split_three(features(code, source, False))
         stack = jnp.concatenate([h, m, h, m, l, h, blank], axis=0).astype(bf16)
-        values = jnp.exp2(mm(near_ref[block], stack))
-        high, low = split_two(values)
-        cov_ref[slot, 0:WIDTH] = high
-        cov_ref[slot, WIDTH:] = low
+        cov_ref[slot] = jnp.exp2(mm(near_ref[block], stack))
 
     def self_tile(step, _):
         for k in range(4):
@@ -217,14 +215,25 @@
     for copy in first:
         copy.wait_recv()
 
-    def packed(rows):
-        high, low = split_two(rows)
-        return jnp.concatenate([high, low], axis=0)
+    def spread(values):
+        tall = jnp.transpose(
+            jnp.concatenate([values, jnp.zeros((WIDTH - BLOCKS, WIDTH), f32)], axis=0)
+        )
+        for block in range(BLOCKS):
+            column_ref[block] = jnp.broadcast_to(tall[:, block : block + 1], (WIDTH, WIDTH))
+
+    def down(slot, block):
+        product = cov_ref[slot] * column_ref[block]
+        return jnp.sum(
+            jnp.sum(product.reshape(WIDTH // SUB, SUB, WIDTH), axis=0), axis=0, keepdims=True
+        )
 
     def doubled(values):
         high, low = split_two(values)
         return jnp.concatenate([high, low], axis=0)
 
+    lanes_sq = lax.broadcasted_iota(jnp.int32, (WIDTH, slots), 1)
+    ones = jnp.ones((2 * WIDTH, WIDTH), bf16)
     in_flight = []
     own_weight = None
     for it in range(ITERS):
@@ -236,22 +245,18 @@
                 copy.start()
             halo_ref[OWN] = vector
 
+        spread(vector)
+
         def pay_step(step, _):
             if it == 0:
                 for k in range(SUB):
                     slot = step * SUB + k
                     code = jnp.minimum(spair_ref[0, 0, slot], CODES - 1)
                     make_tile(slot, spair_ref[2, 0, slot], code, spair_ref[1, 0, slot])
-            rows = jnp.zeros((SUB, WIDTH), f32)
-            for k in range(SUB):
-                block = spair_ref[2, 0, step * SUB + k]
-                rows = jnp.where(sub == k, basis_ref[it, pl.ds(block, 1), :], rows)
-            left = packed(rows)
-            left = jnp.concatenate([left, left], axis=1)
             total = jnp.zeros((SUB, WIDTH), f32)
             for k in range(SUB):
-                out = mm(left, cov_ref[step * SUB + k])
-                total = jnp.where(sub == k, out[:SUB] + out[SUB:], total)
+                slot = step * SUB + k
+                total = jnp.where(sub == k, down(slot, spair_ref[2, 0, slot]), total)
             pay_ref[pl.ds(step * SUB, SUB), :] = total
             return 0
 
@@ -271,12 +276,10 @@
             copy.start()
 
         def self_step(step, _):
-            left = packed(basis_ref[it, pl.ds(step * SUB, SUB), :])
-            left = jnp.concatenate([left, left], axis=1)
             total = jnp.zeros((SUB, WIDTH), f32)
             for k in range(SUB):
-                out = mm(left, cov_ref[slots + step * SUB + k])
-                total = jnp.where(sub == k, out[:SUB] + out[SUB:], total)
+                block = step * SUB + k
+                total = jnp.where(sub == k, down(slots + block, block), total)
             self_ref[pl.ds(step * SUB, SUB), :] = total
             return 0
 
@@ -284,23 +287,24 @@
         for copy in arriving:
             copy.wait_recv()
 
-        def gain_step(step, _):
-            rows = jnp.zeros((SUB, WIDTH), f32)
+        def gain_step(step, tall):
             for k in range(SUB):
                 slot = step * SUB + k
                 code = jnp.minimum(spair_ref[0, 0, slot], CODES - 1)
-                rows = jnp.where(sub == k, halo_ref[code, pl.ds(spair_ref[1, 0, slot], 1), :], rows)
-            left = packed(rows)
-            total = jnp.zeros((SUB, WIDTH), f32)
-            for k in range(SUB):
-                out = mm_trans(left, cov_ref[step * SUB + k])
-                out = out[:SUB] + out[SUB:]
-                total = jnp.where(sub == k, out[:, :WIDTH] + out[:, WIDTH:], total)
-            gain_ref[pl.ds(step * SUB, SUB), :] = total
-            return 0
-
-        lax.fori_loop(0, slots // SUB, gain_step, 0)
-        totals = mm(onto_ref[...], doubled(gain_ref[...])) + owed_ref[it, OWN, 0:BLOCKS]
+                row = halo_ref[code, pl.ds(spair_ref[1, 0, slot], 1), :]
+                product = cov_ref[slot] * row
+                if k in BY_UNIT:
+                    high, low = split_two(product)
+                    reach = mm(jnp.concatenate([high, low], axis=1), ones)
+                else:
+                    reach = jnp.sum(product, axis=1, keepdims=True)
+                tall = jnp.where(lanes_sq == slot, reach, tall)
+            return tall
+
+        tall = lax.fori_loop(0, slots // SUB, gain_step, jnp.zeros((WIDTH, slots), f32))
+        high, low = split_two(tall)
+        totals = mm_trans(onto_ref[...], jnp.concatenate([high, low], axis=1))
+        totals = totals + owed_ref[it, OWN, 0:BLOCKS]
         for copy in returns:
             copy.wait_recv()
         for c in sides:
@@ -405,14 +409,14 @@
             pltpu.VMEM((3, 1, slots), jnp.int32),
             pltpu.SMEM((3, 1, slots), jnp.int32),
             pltpu.VMEM((BLOCKS, WIDTH, WIDTH), bf16),
-            pltpu.VMEM((slots + BLOCKS, 2 * WIDTH, WIDTH), bf16),
+            pltpu.VMEM((slots + BLOCKS, WIDTH, WIDTH), f32),
+            pltpu.VMEM((BLOCKS, WIDTH, WIDTH), f32),
             pltpu.VMEM((CODES, 3, BLOCKS, WIDTH), f32),
             pltpu.VMEM((CODES, BLOCKS, WIDTH), f32),
             pltpu.VMEM((CODES, BLOCKS, WIDTH), f32),
             pltpu.VMEM((CODES, BLOCKS, WIDTH), f32),
             pltpu.VMEM((ITERS, CODES, 2 * BLOCKS, WIDTH), f32),
             pltpu.VMEM((ITERS, CODES, 2 * BLOCKS, WIDTH), f32),
-            pltpu.VMEM((slots, WIDTH), f32),
             pltpu.VMEM((slots, WIDTH), f32),
             pltpu.VMEM((BLOCKS, WIDTH), f32),
             pltpu.VMEM((ITERS + 1, BLOCKS, WIDTH), f32),

time: 60.7 us -> 56.9 us (0.937)
  Pallas kernels: 58.7 us -> 54.9 us
    pallas_call x1, Pallas kernels: 58.7 us -> 54.9 us  [local(): pl.pallas_call(functools.partial(body, slots), out_shape=(shape, shape),...]
where the time goes in v3:
time: 56.9 us; the launch traced here: 56.7 us
  Pallas kernels  54.9 us (96%)
  local copies, waits for them, and re-layouts  1.21 us (2%)
  between operations  0.64 us (1%)
    pallas_call x1, Pallas kernels, local(): pl.pallas_call(functools.partial(body, slots), out_shape=(shape, shape),...  54.9 us
    unnamed x2, local copies, waits for them, and re-layouts  1.21 us

profile of v3, /device:TPU:1, one launch (start us, length us, event | category | flops | bytes accessed | tf_op | source)
XLA Modules:
  0.0 56.7 jit_solution(17569741472373316669)
XLA Ops:
  0.6 54.9 %shard_map.68 = (f32[32,128]{1,0:T(8,128)S(1)}, f32[32,128]{1,0:T(8,128)S(1)}) custom-call(f32[1,1,32,128]{3,2,1,0:T(8,128)} %delta_in.1, f32[1,1,32,128]{3,2,1,0:T(8,128)} %noise_in.1, f32[1,1,3,32,128]{4,3,2,1,0:T(8,128)} %pos_in.1, s32[1,1,32]{2,1,0:T(1,128)} %count_in.1, s32[1,3,1,128]{3,2,1,0:T(1,128)} %bitcast.5), custom_call_target="tpu_custom_call" | custom-call | tf_op jit(solution)/shard_map/pallas_call | solution.py:399
  55.5 0.6 %copy.9 = f32[1,1,32,128]{3,2,1,0:T(8,128)} copy(f32[1,1,32,128]{3,2,1,0:T(8,128)S(1)} %bitcast.4) | data formatting | bytes 32768
  56.1 0.6 %copy.10 = f32[1,1,32,128]{3,2,1,0:T(8,128)} copy(f32[1,1,32,128]{3,2,1,0:T(8,128)S(1)} %bitcast.3) | data formatting | bytes 32768

commit v4 on v3

--- a/solution.py
+++ b/solution.py
@@ -14,7 +14,6 @@
 OWN = 4
 SUB = 8
 INNER = 8
-BY_UNIT = (1, 4, 7)
 
 signal_amp = 0.25
 bf16 = jnp.bfloat16
@@ -45,9 +44,9 @@
     slots,
     delta_in, noise_in, pos_in, count_in, pair_in,
     field_ref, resid_ref,
-    delta_ref, noise_ref, pos_ref, count_ref, pair_ref, spair_ref,
-    near_ref, cov_ref, column_ref, first_ref, halo0_ref, halo1_ref, halo2_ref, owed_ref, got_ref,
-    pay_ref, self_ref, basis_ref, image_ref, onto_ref, from_ref,
+    delta_ref, noise_ref, pos_ref, count_ref, pair_ref, order_ref, spair_ref,
+    near_ref, cov_ref, running_ref, column_ref, first_ref, halo0_ref, halo1_ref, halo2_ref, owed_ref, got_ref,
+    pay_ref, self_ref, basis_ref, image_ref, from_ref,
     sum_ref, red1_ref, red2_ref, red3_ref,
     load_sem, first_send, first_recv, halo_send, halo_recv, owed_send, owed_recv,
     red1_send, red1_recv, red2_send, red2_recv, red3_send, red3_recv,
@@ -86,7 +85,6 @@
             (
                 (pos_in.at[0, 0], pos_ref),
                 (pair_in.at[0], pair_ref),
-                (pair_in.at[0], spair_ref),
                 (count_in.at[0], count_ref),
                 (noise_in.at[0, 0], noise_ref),
                 (delta_in.at[0, 0], delta_ref),
@@ -147,20 +145,37 @@
         copy.start()
     halo0_ref[OWN] = basis_ref[0]
 
+    shape = (slots, slots)
+    rows_s = lax.broadcasted_iota(jnp.int32, shape, 0)
+    lanes_s = lax.broadcasted_iota(jnp.int32, shape, 1)
     codes = pair_ref[0]
     near_row = (codes >= 3).astype(jnp.int32) + (codes >= 6).astype(jnp.int32)
     row_s = me_s + near_row - 1
     row_g = me_g + (codes - 3 * near_row) - 1
     filled = codes < CODES
     inside = filled & (row_s >= 0) & (row_s < n_sky) & (row_g >= 0) & (row_g < n_gz)
-    flat = jnp.minimum(codes, CODES - 1) * BLOCKS + pair_ref[1]
     target = pair_ref[2]
-    weight = jnp.where(inside, signal_amp, 0.0)
-    rows_b = lax.broadcasted_iota(jnp.int32, (BLOCKS, slots), 0)
-    hits = rows_b == target
-    onto = jnp.where(hits, weight, 0.0)
-    onto_ref[:, :slots] = onto.astype(bf16)
-    onto_ref[:, slots:] = onto.astype(bf16)
+    target_col = jnp.sum(jnp.where(rows_s == lanes_s, target, 0), axis=1, keepdims=True)
+    before = (target < target_col) | ((target == target_col) & (lanes_s < rows_s))
+    rank = jnp.sum(before.astype(jnp.int32), axis=1, keepdims=True)
+    place = rank == lanes_s
+    fields = (jnp.minimum(codes, CODES - 1), pair_ref[1], target, inside.astype(jnp.int32))
+    limits = (CODES - 1, BLOCKS - 1, BLOCKS - 1, 1)
+    sub = lax.broadcasted_iota(jnp.int32, (SUB, slots), 0)
+    table = jnp.zeros((SUB, slots), jnp.int32)
+    for i, (field, limit) in enumerate(zip(fields, limits)):
+        column = jnp.sum(jnp.where(rows_s == lanes_s, field, 0), axis=1, keepdims=True)
+        moved = jnp.sum(jnp.where(place, column, 0), axis=0, keepdims=True)
+        table = jnp.where(sub == i, jnp.clip(moved, 0, limit), table)
+    ends = jnp.sum((target_col <= lanes_s).astype(jnp.int32), axis=0, keepdims=True)
+    table = jnp.where(sub == len(fields), jnp.clip(ends, 0, slots), table)
+    order_ref[...] = table
+    to_scalar = pltpu.make_async_copy(order_ref, spair_ref, load_sem.at[5])
+    to_scalar.start()
+
+    flat = table[0:1] * BLOCKS + table[1:2]
+    weight = table[3:4].astype(f32) * signal_amp
+    hits = lax.broadcasted_iota(jnp.int32, (BLOCKS, slots), 0) == target
     named = jnp.sum(
         jnp.where(hits & filled, signal_amp, 0.0), axis=1, keepdims=True
     )
@@ -177,8 +192,6 @@
     mid_x = (2 * me_s + 1).astype(f32)
     mid_z = (4 * me_g + 2).astype(f32)
     scale = math.sqrt(math.log2(math.e))
-    sub = lax.broadcasted_iota(jnp.int32, (SUB, WIDTH), 0)
-
     def features(code, block, swap):
         x = (first_ref[code, 0, pl.ds(block, 1), :] - mid_x) * scale
         y = (first_ref[code, 1, pl.ds(block, 1), :] - 1.0) * scale
@@ -212,15 +225,15 @@
         return 0
 
     lax.fori_loop(0, BLOCKS // 4, self_tile, 0)
+    to_scalar.wait()
     for copy in first:
         copy.wait_recv()
 
     def spread(values):
-        tall = jnp.transpose(
-            jnp.concatenate([values, jnp.zeros((WIDTH - BLOCKS, WIDTH), f32)], axis=0)
-        )
         for block in range(BLOCKS):
-            column_ref[block] = jnp.broadcast_to(tall[:, block : block + 1], (WIDTH, WIDTH))
+            column_ref[block] = jnp.transpose(
+                jnp.broadcast_to(values[block : block + 1], (WIDTH, WIDTH))
+            )
 
     def down(slot, block):
         product = cov_ref[slot] * column_ref[block]
@@ -232,8 +245,7 @@
         high, low = split_two(values)
         return jnp.concatenate([high, low], axis=0)
 
-    lanes_sq = lax.broadcasted_iota(jnp.int32, (WIDTH, slots), 1)
-    ones = jnp.ones((2 * WIDTH, WIDTH), bf16)
+    lanes_sq = lax.broadcasted_iota(jnp.int32, (WIDTH, WIDTH), 1)
     in_flight = []
     own_weight = None
     for it in range(ITERS):
@@ -251,12 +263,11 @@
             if it == 0:
                 for k in range(SUB):
                     slot = step * SUB + k
-                    code = jnp.minimum(spair_ref[0, 0, slot], CODES - 1)
-                    make_tile(slot, spair_ref[2, 0, slot], code, spair_ref[1, 0, slot])
+                    make_tile(slot, spair_ref[2, slot], spair_ref[0, slot], spair_ref[1, slot])
             total = jnp.zeros((SUB, WIDTH), f32)
             for k in range(SUB):
                 slot = step * SUB + k
-                total = jnp.where(sub == k, down(slot, spair_ref[2, 0, slot]), total)
+                total = jnp.where(sub == k, down(slot, spair_ref[2, slot]), total)
             pay_ref[pl.ds(step * SUB, SUB), :] = total
             return 0
 
@@ -287,23 +298,25 @@
         for copy in arriving:
             copy.wait_recv()
 
-        def gain_step(step, tall):
+        def gain_step(step, running):
             for k in range(SUB):
                 slot = step * SUB + k
-                code = jnp.minimum(spair_ref[0, 0, slot], CODES - 1)
-                row = halo_ref[code, pl.ds(spair_ref[1, 0, slot], 1), :]
-                product = cov_ref[slot] * row
-                if k in BY_UNIT:
-                    high, low = split_two(product)
-                    reach = mm(jnp.concatenate([high, low], axis=1), ones)
-                else:
-                    reach = jnp.sum(product, axis=1, keepdims=True)
-                tall = jnp.where(lanes_sq == slot, reach, tall)
-            return tall
-
-        tall = lax.fori_loop(0, slots // SUB, gain_step, jnp.zeros((WIDTH, slots), f32))
-        high, low = split_two(tall)
-        totals = mm_trans(onto_ref[...], jnp.concatenate([high, low], axis=1))
+                row = halo_ref[spair_ref[0, slot], pl.ds(spair_ref[1, slot], 1), :]
+                row = row * (spair_ref[3, slot].astype(f32) * signal_amp)
+                same = spair_ref[2, slot] == spair_ref[2, jnp.maximum(slot - 1, 0)]
+                running = running * same.astype(f32) + cov_ref[slot] * row
+                running_ref[slot] = running
+            return running
+
+        lax.fori_loop(0, slots // SUB, gain_step, jnp.zeros((WIDTH, WIDTH), f32))
+        tall = jnp.zeros((WIDTH, WIDTH), f32)
+        for block in range(BLOCKS):
+            end = spair_ref[4, block]
+            start = spair_ref[4, block - 1] if block > 0 else 0
+            reach = jnp.sum(running_ref[jnp.clip(end - 1, 0, slots - 1)], axis=1, keepdims=True)
+            reach = reach * (end > start).astype(f32)
+            tall = jnp.where(lanes_sq == block, reach, tall)
+        totals = jnp.transpose(tall)[:BLOCKS]
         totals = totals + owed_ref[it, OWN, 0:BLOCKS]
         for copy in returns:
             copy.wait_recv()
@@ -407,9 +420,11 @@
             pltpu.VMEM((3, BLOCKS, WIDTH), f32),
             pltpu.VMEM((1, BLOCKS), jnp.int32),
             pltpu.VMEM((3, 1, slots), jnp.int32),
-            pltpu.SMEM((3, 1, slots), jnp.int32),
+            pltpu.VMEM((SUB, slots), jnp.int32),
+            pltpu.SMEM((SUB, slots), jnp.int32),
             pltpu.VMEM((BLOCKS, WIDTH, WIDTH), bf16),
             pltpu.VMEM((slots + BLOCKS, WIDTH, WIDTH), f32),
+            pltpu.VMEM((slots, WIDTH, WIDTH), f32),
             pltpu.VMEM((BLOCKS, WIDTH, WIDTH), f32),
             pltpu.VMEM((CODES, 3, BLOCKS, WIDTH), f32),
             pltpu.VMEM((CODES, BLOCKS, WIDTH), f32),
@@ -421,7 +436,6 @@
             pltpu.VMEM((BLOCKS, WIDTH), f32),
             pltpu.VMEM((ITERS + 1, BLOCKS, WIDTH), f32),
             pltpu.VMEM((ITERS + 1, BLOCKS, WIDTH), f32),
-            pltpu.VMEM((BLOCKS, 2 * slots), bf16),
             pltpu.VMEM((CODES * BLOCKS, 2 * slots), bf16),
             pltpu.VMEM((3, SUB, WIDTH), f32),
             pltpu.VMEM((n_gz - 1, SUB, WIDTH), f32),

time: 56.9 us -> 54 us (0.949)
  Pallas kernels: 54.9 us -> 52 us
    pallas_call x1, Pallas kernels: 54.9 us -> 52 us  [local(): pl.pallas_call(functools.partial(body, slots), out_shape=(shape, shape),...]
where the time goes in v4:
time: 54 us; the launch traced here: 53.8 us
  Pallas kernels  52 us (96%)
  local copies, waits for them, and re-layouts  1.21 us (2%)
  between operations  0.64 us (1%)
    pallas_call x1, Pallas kernels, local(): pl.pallas_call(functools.partial(body, slots), out_shape=(shape, shape),...  52 us
    unnamed x2, local copies, waits for them, and re-layouts  1.21 us

profile of v4, /device:TPU:1, one launch (start us, length us, event | category | flops | bytes accessed | tf_op | source)
XLA Modules:
  0.0 53.8 jit_solution(15373530991058181074)
XLA Ops:
  0.6 52.0 %shard_map.68 = (f32[32,128]{1,0:T(8,128)S(1)}, f32[32,128]{1,0:T(8,128)S(1)}) custom-call(f32[1,1,32,128]{3,2,1,0:T(8,128)} %delta_in.1, f32[1,1,32,128]{3,2,1,0:T(8,128)} %noise_in.1, f32[1,1,3,32,128]{4,3,2,1,0:T(8,128)} %pos_in.1, s32[1,1,32]{2,1,0:T(1,128)} %count_in.1, s32[1,3,1,128]{3,2,1,0:T(1,128)} %bitcast.5), custom_call_target="tpu_custom_call" | custom-call | tf_op jit(solution)/shard_map/pallas_call | solution.py:412
  52.6 0.6 %copy.9 = f32[1,1,32,128]{3,2,1,0:T(8,128)} copy(f32[1,1,32,128]{3,2,1,0:T(8,128)S(1)} %bitcast.4) | data formatting | bytes 32768
  53.2 0.6 %copy.10 = f32[1,1,32,128]{3,2,1,0:T(8,128)} copy(f32[1,1,32,128]{3,2,1,0:T(8,128)S(1)} %bitcast.3) | data formatting | bytes 32768

commit v5 on v4

--- a/solution.py
+++ b/solution.py
@@ -74,9 +74,9 @@
     def outer_at(step):
         return ((outer + step) % n_outer * INNER + inner, me_g)
 
-    sides = [code for code in range(CODES) if code != OWN]
+    sides = (0, 2, 6, 8, 1, 7, 3, 5)
     partners = [tile_at(code) for code in sides]
-    partners += [gz_at(step) for step in range(1, n_gz)]
+    partners += [gz_at(step) for step in range(2, n_gz - 1)]
     partners += [inner_at(step) for step in range(1, INNER)]
     partners += [outer_at(step) for step in range(1, n_outer)]
     loads = [
@@ -105,8 +105,37 @@
             device_id=device, device_id_type=pl.DeviceIdType.MESH,
         )
 
-    for copy in loads:
-        copy.wait()
+    loads[0].wait()
+    first_ref[OWN] = pos_ref[...]
+
+    sub = lax.broadcasted_iota(jnp.int32, (SUB, WIDTH), 0)
+    mid_x = (2 * me_s + 1).astype(f32)
+    mid_z = (4 * me_g + 2).astype(f32)
+    scale = math.sqrt(math.log2(math.e))
+    def features(code, block, swap):
+        x = (first_ref[code, 0, pl.ds(block, 1), :] - mid_x) * scale
+        y = (first_ref[code, 1, pl.ds(block, 1), :] - 1.0) * scale
+        z = (first_ref[code, 2, pl.ds(block, 1), :] - mid_z) * scale
+        size = -0.5 * (x * x + y * y + z * z)
+        tile = jnp.where(sub == 0, x, 0.0)
+        tile = jnp.where(sub == 1, y, tile)
+        tile = jnp.where(sub == 2, z, tile)
+        tile = jnp.where(sub == (3 if swap else 4), size, tile)
+        return jnp.where(sub == (4 if swap else 3), 1.0, tile)
+
+    blank = jnp.zeros((WIDTH - 6 * SUB, WIDTH), f32)
+    depth = 6 * SUB
+
+    def near_step(step, _):
+        for k in range(4):
+            block = step * 4 + k
+            h, m, l = split_three(features(OWN, block, True))
+            stack = jnp.concatenate([h, h, m, m, h, l, blank], axis=0)
+            near_ref[block] = jnp.transpose(stack).astype(bf16)
+        return 0
+
+    lax.fori_loop(0, BLOCKS // 4, near_step, 0)
+
     pl.semaphore_wait(barrier, len(partners))
     first = [
         remote(pos_ref, first_ref.at[8 - c], first_send.at[c], first_recv.at[8 - c], tile_at(c))
@@ -114,7 +143,8 @@
     ]
     for copy in first:
         copy.start()
-    first_ref[OWN] = pos_ref[...]
+    for copy in loads[1:]:
+        copy.wait()
 
     def halo_copies(it, into):
         return [
@@ -161,7 +191,6 @@
     place = rank == lanes_s
     fields = (jnp.minimum(codes, CODES - 1), pair_ref[1], target, inside.astype(jnp.int32))
     limits = (CODES - 1, BLOCKS - 1, BLOCKS - 1, 1)
-    sub = lax.broadcasted_iota(jnp.int32, (SUB, slots), 0)
     table = jnp.zeros((SUB, slots), jnp.int32)
     for i, (field, limit) in enumerate(zip(fields, limits)):
         column = jnp.sum(jnp.where(rows_s == lanes_s, field, 0), axis=1, keepdims=True)
@@ -189,34 +218,18 @@
     for c in range(CODES):
         owed_ref[0, c, BLOCKS:] = sourced[c * BLOCKS : (c + 1) * BLOCKS]
 
-    mid_x = (2 * me_s + 1).astype(f32)
-    mid_z = (4 * me_g + 2).astype(f32)
-    scale = math.sqrt(math.log2(math.e))
-    def features(code, block, swap):
-        x = (first_ref[code, 0, pl.ds(block, 1), :] - mid_x) * scale
-        y = (first_ref[code, 1, pl.ds(block, 1), :] - 1.0) * scale
-        z = (first_ref[code, 2, pl.ds(block, 1), :] - mid_z) * scale
-        size = -0.5 * (x * x + y * y + z * z)
-        tile = jnp.where(sub == 0, x, 0.0)
-        tile = jnp.where(sub == 1, y, tile)
-        tile = jnp.where(sub == 2, z, tile)
-        tile = jnp.where(sub == (3 if swap else 4), size, tile)
-        return jnp.where(sub == (4 if swap else 3), 1.0, tile)
-
-    blank = jnp.zeros((WIDTH - 6 * SUB, WIDTH), f32)
-
-    def near_step(block, _):
-        h, m, l = split_three(features(OWN, block, True))
-        stack = jnp.concatenate([h, h, m, m, h, l, blank], axis=0)
-        near_ref[block] = jnp.transpose(stack).astype(bf16)
-        return 0
-
-    lax.fori_loop(0, BLOCKS, near_step, 0)
+    def spread(values):
+        for block in range(BLOCKS):
+            column_ref[block] = jnp.transpose(
+                jnp.broadcast_to(values[block : block + 1], (WIDTH, WIDTH))
+            )
+
+    spread(basis_ref[0])
 
     def make_tile(slot, block, code, source):
         h, m, l = split_three(features(code, source, False))
-        stack = jnp.concatenate([h, m, h, m, l, h, blank], axis=0).astype(bf16)
-        cov_ref[slot] = jnp.exp2(mm(near_ref[block], stack))
+        stack = jnp.concatenate([h, m, h, m, l, h], axis=0).astype(bf16)
+        cov_ref[slot] = jnp.exp2(mm(near_ref[block, :, :depth], stack))
 
     def self_tile(step, _):
         for k in range(4):
@@ -228,12 +241,6 @@
     to_scalar.wait()
     for copy in first:
         copy.wait_recv()
-
-    def spread(values):
-        for block in range(BLOCKS):
-            column_ref[block] = jnp.transpose(
-                jnp.broadcast_to(values[block : block + 1], (WIDTH, WIDTH))
-            )
 
     def down(slot, block):
         product = cov_ref[slot] * column_ref[block]
@@ -257,13 +264,20 @@
                 copy.start()
             halo_ref[OWN] = vector
 
-        spread(vector)
+        if it > 0:
+            spread(vector)
+
+        if it == 0:
+
+            def pair_tile(step, _):
+                for k in range(32):
+                    slot = step * 32 + k
+                    make_tile(slot, spair_ref[2, slot], spair_ref[0, slot], spair_ref[1, slot])
+                return 0
+
+            lax.fori_loop(0, slots // 32, pair_tile, 0)
 
         def pay_step(step, _):
-            if it == 0:
-                for k in range(SUB):
-                    slot = step * SUB + k
-                    make_tile(slot, spair_ref[2, slot], spair_ref[0, slot], spair_ref[1, slot])
             total = jnp.zeros((SUB, WIDTH), f32)
             for k in range(SUB):
                 slot = step * SUB + k

time: 54 us -> 51.3 us (0.950)
  Pallas kernels: 52 us -> 49.3 us
    pallas_call x1, Pallas kernels: 52 us -> 49.3 us  [local(): pl.pallas_call(functools.partial(body, slots), out_shape=(shape, shape),...]
where the time goes in v5:
time: 51.3 us; the launch traced here: 51.2 us
  Pallas kernels  49.3 us (96%)
  local copies, waits for them, and re-layouts  1.21 us (2%)
  between operations  0.64 us (1%)
    pallas_call x1, Pallas kernels, local(): pl.pallas_call(functools.partial(body, slots), out_shape=(shape, shape),...  49.3 us
    unnamed x2, local copies, waits for them, and re-layouts  1.21 us

profile of v5, /device:TPU:1, one launch (start us, length us, event | category | flops | bytes accessed | tf_op | source)
XLA Modules:
  0.0 51.2 jit_solution(7791578893008202294)
XLA Ops:
  0.6 49.3 %shard_map.68 = (f32[32,128]{1,0:T(8,128)S(1)}, f32[32,128]{1,0:T(8,128)S(1)}) custom-call(f32[1,1,32,128]{3,2,1,0:T(8,128)} %delta_in.1, f32[1,1,32,128]{3,2,1,0:T(8,128)} %noise_in.1, f32[1,1,3,32,128]{4,3,2,1,0:T(8,128)} %pos_in.1, s32[1,1,32]{2,1,0:T(1,128)} %count_in.1, s32[1,3,1,128]{3,2,1,0:T(1,128)} %bitcast.5), custom_call_target="tpu_custom_call" | custom-call | tf_op jit(solution)/shard_map/pallas_call | solution.py:426
  50.0 0.6 %copy.9 = f32[1,1,32,128]{3,2,1,0:T(8,128)} copy(f32[1,1,32,128]{3,2,1,0:T(8,128)S(1)} %bitcast.4) | data formatting | bytes 32768
  50.6 0.6 %copy.10 = f32[1,1,32,128]{3,2,1,0:T(8,128)} copy(f32[1,1,32,128]{3,2,1,0:T(8,128)S(1)} %bitcast.3) | data formatting | bytes 32768

commit v6 on v5

--- a/solution.py
+++ b/solution.py
@@ -43,7 +43,7 @@
 def body(
     slots,
     delta_in, noise_in, pos_in, count_in, pair_in,
-    field_ref, resid_ref,
+    out_ref,
     delta_ref, noise_ref, pos_ref, count_ref, pair_ref, order_ref, spair_ref,
     near_ref, cov_ref, running_ref, column_ref, first_ref, halo0_ref, halo1_ref, halo2_ref, owed_ref, got_ref,
     pay_ref, self_ref, basis_ref, image_ref, from_ref,
@@ -253,7 +253,8 @@
         return jnp.concatenate([high, low], axis=0)
 
     lanes_sq = lax.broadcasted_iota(jnp.int32, (WIDTH, WIDTH), 1)
-    in_flight = []
+    ones = jnp.ones((2 * WIDTH, WIDTH), bf16)
+    in_flight = first
     own_weight = None
     for it in range(ITERS):
         vector = basis_ref[it]
@@ -327,7 +328,12 @@
         for block in range(BLOCKS):
             end = spair_ref[4, block]
             start = spair_ref[4, block - 1] if block > 0 else 0
-            reach = jnp.sum(running_ref[jnp.clip(end - 1, 0, slots - 1)], axis=1, keepdims=True)
+            sums = running_ref[jnp.clip(end - 1, 0, slots - 1)]
+            if block % 3 == 0:
+                high, low = split_two(sums)
+                reach = mm(jnp.concatenate([high, low], axis=1), ones)
+            else:
+                reach = jnp.sum(sums, axis=1, keepdims=True)
             reach = reach * (end > start).astype(f32)
             tall = jnp.where(lanes_sq == block, reach, tall)
         totals = jnp.transpose(tall)[:BLOCKS]
@@ -344,7 +350,7 @@
         image = live * totals + noise * vector
         image_ref[it + 1] = image
         basis_ref[it + 1] = precond * image
-        in_flight += arriving + returns
+        in_flight = in_flight + arriving + returns
 
     moments = jnp.zeros((SUB, WIDTH), f32)
     for m in range(2 * ITERS + 1):
@@ -366,10 +372,12 @@
         ]
         for copy in copies:
             copy.start()
+        for copy in in_flight:
+            copy.wait_send()
+        in_flight = copies
         for step, copy in enumerate(copies):
             copy.wait_recv()
             moments = moments + into[step]
-        in_flight += copies
     total = jnp.sum(moments, axis=1, keepdims=True)
     mu = [total[m : m + 1] for m in range(2 * ITERS + 1)]
 
@@ -408,9 +416,9 @@
     out_resid = image_ref[0]
     for i in range(1, ITERS + 1):
         out_resid = out_resid + resid[i] * image_ref[i]
-    field_ref[...] = out_field
-    resid_ref[...] = out_resid
-    for copy in first + in_flight:
+    out_ref[0] = out_field
+    out_ref[1] = out_resid
+    for copy in in_flight:
         copy.wait_send()
 
 
@@ -421,13 +429,13 @@
     n_outer = n_sky // INNER
     vmem = pl.BlockSpec(memory_space=pltpu.VMEM)
     hbm = pl.BlockSpec(memory_space=pltpu.HBM)
-    shape = jax.ShapeDtypeStruct((BLOCKS, WIDTH), f32)
+    shape = jax.ShapeDtypeStruct((2, BLOCKS, WIDTH), f32)
     dma = pltpu.SemaphoreType.DMA
-    field, resid = pl.pallas_call(
+    both = pl.pallas_call(
         functools.partial(body, slots),
-        out_shape=(shape, shape),
+        out_shape=shape,
         in_specs=[hbm] * 5,
-        out_specs=(vmem, vmem),
+        out_specs=vmem,
         scratch_shapes=[
             pltpu.VMEM((BLOCKS, WIDTH), f32),
             pltpu.VMEM((BLOCKS, WIDTH), f32),
@@ -473,7 +481,7 @@
             )
         )
     )
-    return field[None, None], resid[None, None]
+    return both[0][None, None], both[1][None, None]
 
 
 def solution(mesh):

time: 51.3 us -> 50.4 us (0.982)
  local copies, waits for them, and re-layouts: 1.21 us -> 0.61 us
    unnamed x2 -> x0, local copies, waits for them, and re-layouts: 1.21 us -> none
    another operation x0 -> x1, local copies, waits for them, and re-layouts: none -> 0.61 us  [local(): return (both[0][None, None], both[1][None, None])]
where the time goes in v6:
time: 50.4 us; the launch traced here: 50.3 us
  Pallas kernels  49 us (97%)
  between operations  0.64 us (1%)
  local copies, waits for them, and re-layouts  0.61 us (1%)
    pallas_call x1, Pallas kernels, local(): pl.pallas_call(functools.partial(body, slots), out_shape=shape, in_specs=...  49 us

profile of v6, /device:TPU:1, one launch (start us, length us, event | category | flops | bytes accessed | tf_op | source)
XLA Modules:
  0.0 50.3 jit_solution(3071393292997900382)
XLA Ops:
  0.6 49.0 %shard_map.68 = f32[2,32,128]{2,1,0:T(8,128)S(1)} custom-call(f32[1,1,32,128]{3,2,1,0:T(8,128)} %delta_in.1, f32[1,1,32,128]{3,2,1,0:T(8,128)} %noise_in.1, f32[1,1,3,32,128]{4,3,2,1,0:T(8,128)} %pos_in.1, s32[1,1,32]{2,1,0:T(1,128)} %count_in.1, s32[1,3,1,128]{3,2,1,0:T(1,128)} %bitcast.5), custom_call_target="tpu_custom_call" | custom-call | tf_op jit(solution)/shard_map/pallas_call | solution.py:434
  49.7 0.6 %slice_bitcast_fusion = (f32[1,1,32,128]{3,2,1,0:T(8,128)}, f32[1,1,32,128]{3,2,1,0:T(8,128)}) fusion(f32[2,32,128]{2,1,0:T(8,128)S(1)} %shard_map.68), kind=kLoop, calls=%fused_computation | loop fusion | bytes 65536 | tf_op jit(solution)/shard_map/broadcast_in_dim;squeeze | solution.py:484

commit v7 on v6

--- a/solution.py
+++ b/solution.py
@@ -170,9 +170,6 @@
     basis_ref[0] = precond * right_side
 
     halo_refs = (halo0_ref, halo1_ref, halo2_ref)
-    arriving = halo_copies(0, halo0_ref)
-    for copy in arriving:
-        copy.start()
     halo0_ref[OWN] = basis_ref[0]
 
     shape = (slots, slots)
@@ -212,11 +209,15 @@
     backs = jnp.where(rows_f == flat, weight, 0.0)
     from_ref[:, :slots] = backs.astype(bf16)
     from_ref[:, slots:] = backs.astype(bf16)
-    sourced = jnp.broadcast_to(
-        jnp.sum(backs, axis=1, keepdims=True), (CODES * BLOCKS, WIDTH)
-    )
+    source_col = jnp.sum(
+        jnp.where(rows_s == lanes_s, table[1:2], 0), axis=1, keepdims=True
+    )
+    by_code = jnp.where(
+        lax.broadcasted_iota(jnp.int32, (2 * SUB, slots), 0) == table[0:1], weight, 0.0
+    )
+    sourced = mm(by_code.astype(bf16), (source_col == lanes_s).astype(bf16))
     for c in range(CODES):
-        owed_ref[0, c, BLOCKS:] = sourced[c * BLOCKS : (c + 1) * BLOCKS]
+        owed_ref[0, c, BLOCKS:] = jnp.broadcast_to(sourced[c : c + 1], (SUB, WIDTH))
 
     def spread(values):
         for block in range(BLOCKS):
@@ -241,6 +242,9 @@
     to_scalar.wait()
     for copy in first:
         copy.wait_recv()
+    arriving = halo_copies(0, halo0_ref)
+    for copy in arriving:
+        copy.start()
 
     def down(slot, block):
         product = cov_ref[slot] * column_ref[block]
@@ -287,10 +291,8 @@
             return 0
 
         lax.fori_loop(0, slots // SUB, pay_step, 0)
-        owed = mm(from_ref[...], doubled(pay_ref[...]))
-        for c in range(CODES):
-            owed_ref[it, c, 0:BLOCKS] = owed[c * BLOCKS : (c + 1) * BLOCKS]
-        extent = 2 * BLOCKS if it == 0 else BLOCKS
+        pays = doubled(pay_ref[...])
+        extent = BLOCKS + SUB if it == 0 else BLOCKS
         returns = [
             remote(
                 owed_ref.at[it, c, pl.ds(0, extent)], got_ref.at[it, 8 - c, pl.ds(0, extent)],
@@ -298,8 +300,10 @@
             )
             for c in sides
         ]
-        for copy in returns:
+        for copy, c in zip(returns, sides):
+            owed_ref[it, c, 0:BLOCKS] = mm(from_ref[c * BLOCKS : (c + 1) * BLOCKS], pays)
             copy.start()
+        owed_ref[it, OWN, 0:BLOCKS] = mm(from_ref[OWN * BLOCKS : (OWN + 1) * BLOCKS], pays)
 
         def self_step(step, _):
             total = jnp.zeros((SUB, WIDTH), f32)
@@ -314,8 +318,8 @@
             copy.wait_recv()
 
         def gain_step(step, running):
-            for k in range(SUB):
-                slot = step * SUB + k
+            for k in range(2 * SUB):
+                slot = step * 2 * SUB + k
                 row = halo_ref[spair_ref[0, slot], pl.ds(spair_ref[1, slot], 1), :]
                 row = row * (spair_ref[3, slot].astype(f32) * signal_amp)
                 same = spair_ref[2, slot] == spair_ref[2, jnp.maximum(slot - 1, 0)]
@@ -323,13 +327,13 @@
                 running_ref[slot] = running
             return running
 
-        lax.fori_loop(0, slots // SUB, gain_step, jnp.zeros((WIDTH, WIDTH), f32))
+        lax.fori_loop(0, slots // SUB // 2, gain_step, jnp.zeros((WIDTH, WIDTH), f32))
         tall = jnp.zeros((WIDTH, WIDTH), f32)
         for block in range(BLOCKS):
             end = spair_ref[4, block]
             start = spair_ref[4, block - 1] if block > 0 else 0
             sums = running_ref[jnp.clip(end - 1, 0, slots - 1)]
-            if block % 3 == 0:
+            if block % 2 == 0:
                 high, low = split_two(sums)
                 reach = mm(jnp.concatenate([high, low], axis=1), ones)
             else:
@@ -343,9 +347,15 @@
         for c in sides:
             totals = totals + got_ref[it, c, 0:BLOCKS]
         if it == 0:
-            own_weight = owed_ref[0, OWN, BLOCKS:] + (signal_amp + named)
+            sources = owed_ref[0, OWN, BLOCKS:]
             for c in sides:
-                own_weight = own_weight + got_ref[0, c, BLOCKS:]
+                sources = sources + got_ref[0, c, BLOCKS:]
+            own_lane = lax.broadcasted_iota(
+                jnp.int32, (BLOCKS, WIDTH), 0
+            ) == lax.broadcasted_iota(jnp.int32, (BLOCKS, WIDTH), 1)
+            own_weight = signal_amp + named + jnp.sum(
+                jnp.where(own_lane, sources[0:1], 0.0), axis=1, keepdims=True
+            )
         totals = totals + own_weight * self_ref[...]
         image = live * totals + noise * vector
         image_ref[it + 1] = image
@@ -452,8 +462,8 @@
             pltpu.VMEM((CODES, BLOCKS, WIDTH), f32),
             pltpu.VMEM((CODES, BLOCKS, WIDTH), f32),
             pltpu.VMEM((CODES, BLOCKS, WIDTH), f32),
-            pltpu.VMEM((ITERS, CODES, 2 * BLOCKS, WIDTH), f32),
-            pltpu.VMEM((ITERS, CODES, 2 * BLOCKS, WIDTH), f32),
+            pltpu.VMEM((ITERS, CODES, BLOCKS + SUB, WIDTH), f32),
+            pltpu.VMEM((ITERS, CODES, BLOCKS + SUB, WIDTH), f32),
             pltpu.VMEM((slots, WIDTH), f32),
             pltpu.VMEM((BLOCKS, WIDTH), f32),
             pltpu.VMEM((ITERS + 1, BLOCKS, WIDTH), f32),

time: 50.4 us -> 50.2 us (level)
  no operation moved by 1% of the time
where the time goes in v7:
time: 50.2 us; the launch traced here: 50.1 us
  Pallas kernels  48.8 us (97%)
  between operations  0.64 us (1%)
  local copies, waits for them, and re-layouts  0.61 us (1%)
    pallas_call x1, Pallas kernels, local(): pl.pallas_call(functools.partial(body, slots), out_shape=shape, in_specs=...  48.8 us

profile of v7, /device:TPU:1, one launch (start us, length us, event | category | flops | bytes accessed | tf_op | source)
XLA Modules:
  0.0 50.1 jit_solution(18377729003355072254)
XLA Ops:
  0.6 48.8 %shard_map.68 = f32[2,32,128]{2,1,0:T(8,128)S(1)} custom-call(f32[1,1,32,128]{3,2,1,0:T(8,128)} %delta_in.1, f32[1,1,32,128]{3,2,1,0:T(8,128)} %noise_in.1, f32[1,1,3,32,128]{4,3,2,1,0:T(8,128)} %pos_in.1, s32[1,1,32]{2,1,0:T(1,128)} %count_in.1, s32[1,3,1,128]{3,2,1,0:T(1,128)} %bitcast.5), custom_call_target="tpu_custom_call" | custom-call | tf_op jit(solution)/shard_map/pallas_call | solution.py:444
  49.5 0.6 %slice_bitcast_fusion = (f32[1,1,32,128]{3,2,1,0:T(8,128)}, f32[1,1,32,128]{3,2,1,0:T(8,128)}) fusion(f32[2,32,128]{2,1,0:T(8,128)S(1)} %shard_map.68), kind=kLoop, calls=%fused_computation | loop fusion | bytes 65536 | tf_op jit(solution)/shard_map/broadcast_in_dim;squeeze | solution.py:494

commit v8 on v7

--- a/solution.py
+++ b/solution.py
@@ -258,6 +258,10 @@
 
     lanes_sq = lax.broadcasted_iota(jnp.int32, (WIDTH, WIDTH), 1)
     ones = jnp.ones((2 * WIDTH, WIDTH), bf16)
+    def with_moment(moments, m):
+        product = basis_ref[m // 2] * image_ref[m - m // 2]
+        return jnp.where(sub == m, jnp.sum(product, axis=0, keepdims=True), moments)
+
     in_flight = first
     own_weight = None
     for it in range(ITERS):
@@ -275,12 +279,12 @@
         if it == 0:
 
             def pair_tile(step, _):
-                for k in range(32):
-                    slot = step * 32 + k
+                for k in range(64):
+                    slot = step * 64 + k
                     make_tile(slot, spair_ref[2, slot], spair_ref[0, slot], spair_ref[1, slot])
                 return 0
 
-            lax.fori_loop(0, slots // 32, pair_tile, 0)
+            lax.fori_loop(0, slots // 64, pair_tile, 0)
 
         def pay_step(step, _):
             total = jnp.zeros((SUB, WIDTH), f32)
@@ -342,6 +346,10 @@
             tall = jnp.where(lanes_sq == block, reach, tall)
         totals = jnp.transpose(tall)[:BLOCKS]
         totals = totals + owed_ref[it, OWN, 0:BLOCKS]
+        if it == ITERS - 1:
+            moments = jnp.zeros((SUB, WIDTH), f32)
+            for m in range(2 * ITERS - 1):
+                moments = with_moment(moments, m)
         for copy in returns:
             copy.wait_recv()
         for c in sides:
@@ -362,10 +370,8 @@
         basis_ref[it + 1] = precond * image
         in_flight = in_flight + arriving + returns
 
-    moments = jnp.zeros((SUB, WIDTH), f32)
-    for m in range(2 * ITERS + 1):
-        product = basis_ref[m // 2] * image_ref[m - m // 2]
-        moments = jnp.where(sub == m, jnp.sum(product, axis=0, keepdims=True), moments)
+    for m in range(2 * ITERS - 1, 2 * ITERS + 1):
+        moments = with_moment(moments, m)
     stages = (
         (gz_at, n_gz, red1_ref, red1_send, red1_recv),
         (inner_at, INNER, red2_ref, red2_send, red2_recv),

time: 50.2 us -> 49.9 us (level)
  no operation moved by 1% of the time
where the time goes in v8:
time: 49.9 us; the launch traced here: 49.7 us
  Pallas kernels  48.5 us (97%)
  between operations  0.64 us (1%)
  local copies, waits for them, and re-layouts  0.61 us (1%)
    pallas_call x1, Pallas kernels, local(): pl.pallas_call(functools.partial(body, slots), out_shape=shape, in_specs=...  48.5 us

profile of v8, /device:TPU:1, one launch (start us, length us, event | category | flops | bytes accessed | tf_op | source)
XLA Modules:
  0.0 49.7 jit_solution(15899346513648702593)
XLA Ops:
  0.6 48.5 %shard_map.68 = f32[2,32,128]{2,1,0:T(8,128)S(1)} custom-call(f32[1,1,32,128]{3,2,1,0:T(8,128)} %delta_in.1, f32[1,1,32,128]{3,2,1,0:T(8,128)} %noise_in.1, f32[1,1,3,32,128]{4,3,2,1,0:T(8,128)} %pos_in.1, s32[1,1,32]{2,1,0:T(1,128)} %count_in.1, s32[1,3,1,128]{3,2,1,0:T(1,128)} %bitcast.5), custom_call_target="tpu_custom_call" | custom-call | tf_op jit(solution)/shard_map/pallas_call | solution.py:450
  49.1 0.6 %slice_bitcast_fusion = (f32[1,1,32,128]{3,2,1,0:T(8,128)}, f32[1,1,32,128]{3,2,1,0:T(8,128)}) fusion(f32[2,32,128]{2,1,0:T(8,128)S(1)} %shard_map.68), kind=kLoop, calls=%fused_computation | loop fusion | bytes 65536 | tf_op jit(solution)/shard_map/broadcast_in_dim;squeeze | solution.py:500

commit v9 on v8

--- a/solution.py
+++ b/solution.py
@@ -322,8 +322,8 @@
             copy.wait_recv()
 
         def gain_step(step, running):
-            for k in range(2 * SUB):
-                slot = step * 2 * SUB + k
+            for k in range(4 * SUB):
+                slot = step * 4 * SUB + k
                 row = halo_ref[spair_ref[0, slot], pl.ds(spair_ref[1, slot], 1), :]
                 row = row * (spair_ref[3, slot].astype(f32) * signal_amp)
                 same = spair_ref[2, slot] == spair_ref[2, jnp.maximum(slot - 1, 0)]
@@ -331,7 +331,7 @@
                 running_ref[slot] = running
             return running
 
-        lax.fori_loop(0, slots // SUB // 2, gain_step, jnp.zeros((WIDTH, WIDTH), f32))
+        lax.fori_loop(0, slots // SUB // 4, gain_step, jnp.zeros((WIDTH, WIDTH), f32))
         tall = jnp.zeros((WIDTH, WIDTH), f32)
         for block in range(BLOCKS):
             end = spair_ref[4, block]

time: 49.9 us -> 49.9 us (level)
  no operation moved by 1% of the time
where the time goes in v9:
time: 49.9 us; the launch traced here: 49.7 us
  Pallas kernels  48.5 us (97%)
  between operations  0.64 us (1%)
  local copies, waits for them, and re-layouts  0.61 us (1%)
    pallas_call x1, Pallas kernels, local(): pl.pallas_call(functools.partial(body, slots), out_shape=shape, in_specs=...  48.5 us

profile of v9, /device:TPU:1, one launch (start us, length us, event | category | flops | bytes accessed | tf_op | source)
XLA Modules:
  0.0 49.7 jit_solution(10618360510626381278)
XLA Ops:
  0.6 48.5 %shard_map.68 = f32[2,32,128]{2,1,0:T(8,128)S(1)} custom-call(f32[1,1,32,128]{3,2,1,0:T(8,128)} %delta_in.1, f32[1,1,32,128]{3,2,1,0:T(8,128)} %noise_in.1, f32[1,1,3,32,128]{4,3,2,1,0:T(8,128)} %pos_in.1, s32[1,1,32]{2,1,0:T(1,128)} %count_in.1, s32[1,3,1,128]{3,2,1,0:T(1,128)} %bitcast.5), custom_call_target="tpu_custom_call" | custom-call | tf_op jit(solution)/shard_map/pallas_call | solution.py:450
  49.1 0.6 %slice_bitcast_fusion = (f32[1,1,32,128]{3,2,1,0:T(8,128)}, f32[1,1,32,128]{3,2,1,0:T(8,128)}) fusion(f32[2,32,128]{2,1,0:T(8,128)S(1)} %shard_map.68), kind=kLoop, calls=%fused_computation | loop fusion | bytes 65536 | tf_op jit(solution)/shard_map/broadcast_in_dim;squeeze | solution.py:500
